TPU v7x, 256 devices: a whole 4x4x8 slice. The times are simulated.
256 devices in a mesh: seq: 16 (over z, core), fsdp: 16 (over y, x).
Axes of the slice: x: 4, y: 4, z: 8, core: 2. Of those that a mesh axis runs over, the one named last changes fastest.
Arguments:
- queries: bfloat16 [3, 16384, 4096], P(None, 'seq', 'fsdp'), may hold values from -6 to 6
- keys: bfloat16 [3, 16384, 4096], P(None, 'seq', 'fsdp'), may hold values from -6 to 6
- values: bfloat16 [3, 16384, 4096], P(None, 'seq', 'fsdp'), may hold values from -6 to 6
- out_grad: bfloat16 [3, 16384, 4096], P(None, 'seq', 'fsdp'), may hold values from -6 to 6
- gain: float32 [3, 4096], P(None, 'fsdp'), may hold values from 0.5 to 1.5
- keep_mask: int32 [3], replicated, may hold values from 0 to 1, as said below
- segments: int32 [16384], P('seq'), may hold values from 0 to 3, never falling along the last dimension, each value on 1 to 8192 neighbouring positions
Outputs:
- query_grad: bfloat16 [3, 16384, 4096], P(None, 'seq', 'fsdp')
- key_grad: bfloat16 [3, 16384, 4096], P(None, 'seq', 'fsdp')
- value_grad: bfloat16 [3, 16384, 4096], P(None, 'seq', 'fsdp')
- gain_grad: float32 [3, 4096], P(None, 'fsdp')
Inputs may be any that keep to these rules, and one draw needn't show every extreme that they name: `segments`: segment numbers never fall along the sequence; a document has 1 to 8192 tokens. `keep_mask`: at least one layer is kept.
All inputs are finite; a program needn't handle non-finite values.
Results may differ from a plain program's by a relative error of at most 0.0058.
Values sent between devices are 32-bit elements; how exact they have to be, the bound alone decides.
A program may use at most 128 MiB of HBM per device.

v0:
```python
import jax
import jax.numpy as jnp
from jax import lax
from jax.sharding import PartitionSpec as P

DH = 128
BLK = 512


EPSILON = 1e-06
KEEP_RATE = 0.75


def entering(shard, axis, combine, identity, reverse):
    count, here = (lax.axis_size(axis), lax.axis_index(axis))
    everything = jax.tree.map(lambda part: lax.all_gather(part, axis), shard)
    start = jax.tree.map(
        lambda part, zero: jnp.broadcast_to(jnp.asarray(zero, part.dtype), part.shape),
        shard,
        identity,
    )

    def step(k, before):
        at = count - 1 - k if reverse else k
        reached = at > here if reverse else at < here
        new = combine(before, jax.tree.map(lambda part: part[at], everything))
        return jax.tree.map(lambda a, b: jnp.where(reached, a, b), new, before)

    return lax.fori_loop(0, count, step, start)


def join_states(first_part, second_part):
    seg_first, state_first = first_part
    seg_second, state_second = second_part
    empty = seg_second < 0
    carried = jnp.logical_or(seg_second == seg_first, empty)
    return (
        jnp.where(empty, seg_first, seg_second),
        state_second + jnp.where(carried, state_first, jnp.float32(0.0)),
    )


def block_prefix(summary_segs, summaries, backward):
    running = (jnp.float32(-1.0), jnp.zeros(summaries.shape[1:], jnp.float32))
    block_total = summaries.shape[0]
    before = [running] * block_total
    block_order = list(range(block_total))
    if backward:
        block_order = block_order[::-1]
    for block_index in block_order:
        before[block_index] = running
        running = join_states(running, (summary_segs[block_index], summaries[block_index]))
    return (before, running)


def local(queries, keys, values, out_grad, gain, keep_mask, segments):
    layer_count, row_count, channels = queries.shape
    head_count = channels // DH
    block_count = row_count // BLK
    feature_count = channels * lax.axis_size("fsdp")
    shape_blocks = (layer_count, block_count, BLK, head_count, DH)
    query_blocks = queries.reshape(shape_blocks)
    key_blocks = keys.reshape(shape_blocks)
    value_blocks = values.reshape(shape_blocks)
    seg_values = segments.astype(jnp.float32).reshape(block_count, BLK)
    places = jnp.arange(BLK)
    causal = places[:, None] >= places[None, :]
    within = jnp.logical_and(causal[None], seg_values[:, :, None] == seg_values[:, None, :])
    tail_select = (seg_values == seg_values[:, -1:])[None, :, :, None, None]
    head_select = (seg_values == seg_values[:, :1])[None, :, :, None, None]
    zero_state = jnp.zeros((layer_count, head_count, DH, DH), jnp.float32)
    identity = (jnp.float32(-1.0), zero_state)
    bf_zero = jnp.zeros((), jnp.bfloat16)
    tails = jnp.einsum(
        "lbshd,lbshe->blhde",
        jnp.where(tail_select, key_blocks, bf_zero),
        value_blocks,
        preferred_element_type=jnp.float32,
    )
    local_before, local_total = block_prefix(seg_values[:, -1], tails, False)
    device_carry = entering(local_total, "seq", join_states, identity, False)
    fwd_joined = [join_states(device_carry, block_carry) for block_carry in local_before]
    fwd_segs = jnp.stack([block_carry[0] for block_carry in fwd_joined])
    fwd_states = jnp.stack([block_carry[1] for block_carry in fwd_joined], 1).astype(jnp.bfloat16)
    seen_fwd = (seg_values == fwd_segs[:, None])[None, :, :, None, None]
    scores = jnp.einsum(
        "lbthd,lbshd->lbhts", query_blocks, key_blocks, preferred_element_type=jnp.float32
    )
    weights = jnp.where(within[None, :, None], scores, 0.0).astype(jnp.bfloat16)
    attention = jnp.einsum(
        "lbhts,lbshd->lbthd", weights, value_blocks, preferred_element_type=jnp.float32
    )
    carried = jnp.einsum(
        "lbthd,lbhde->lbthe", query_blocks, fwd_states, preferred_element_type=jnp.float32
    )
    attention = (attention + jnp.where(seen_fwd, carried, 0.0)).reshape(
        layer_count, row_count, channels
    )
    keep_scale = (keep_mask.astype(jnp.float32) / KEEP_RATE)[:, None, None]
    upstream = out_grad.astype(jnp.float32)
    weighted = upstream * gain[:, None, :]
    local_squares = jnp.sum(attention * attention, -1)
    total_squares = lax.psum(local_squares, "fsdp")
    inverse = 1.0 / jnp.sqrt(total_squares / feature_count + EPSILON)
    normed = attention * inverse[..., None]
    cross = lax.psum(jnp.sum(weighted * normed, -1), "fsdp")
    d_values = keep_scale * (
        inverse[..., None] * weighted - normed * (inverse * cross / feature_count)[..., None]
    )
    d_attention = d_values.astype(jnp.bfloat16)
    gain_part = keep_scale[:, 0] * jnp.sum(upstream * normed, 1)
    gain_grad = lax.psum(gain_part, "seq")
    grad_blocks = d_attention.reshape(shape_blocks)
    fronts = jnp.einsum(
        "lbthd,lbthe->blhde",
        jnp.where(head_select, query_blocks, bf_zero),
        grad_blocks,
        preferred_element_type=jnp.float32,
    )
    local_after, local_front = block_prefix(seg_values[:, 0], fronts, True)
    device_later = entering(local_front, "seq", join_states, identity, True)
    bwd_joined = [join_states(device_later, block_carry) for block_carry in local_after]
    bwd_segs = jnp.stack([block_carry[0] for block_carry in bwd_joined])
    bwd_states = jnp.stack([block_carry[1] for block_carry in bwd_joined], 1).astype(jnp.bfloat16)
    seen_bwd = (seg_values == bwd_segs[:, None])[None, :, :, None, None]
    grad_scores = jnp.einsum(
        "lbthd,lbshd->lbhts", grad_blocks, value_blocks, preferred_element_type=jnp.float32
    )
    grad_weights = jnp.where(within[None, :, None], grad_scores, 0.0).astype(jnp.bfloat16)
    query_part = jnp.einsum(
        "lbhts,lbshd->lbthd", grad_weights, key_blocks, preferred_element_type=jnp.float32
    )
    query_part = query_part + jnp.where(
        seen_fwd,
        jnp.einsum(
            "lbthe,lbhde->lbthd", grad_blocks, fwd_states, preferred_element_type=jnp.float32
        ),
        0.0,
    )
    key_part = jnp.einsum(
        "lbhts,lbthd->lbshd", grad_weights, query_blocks, preferred_element_type=jnp.float32
    )
    key_part = key_part + jnp.where(
        seen_bwd,
        jnp.einsum(
            "lbshe,lbhde->lbshd", value_blocks, bwd_states, preferred_element_type=jnp.float32
        ),
        0.0,
    )
    value_part = jnp.einsum(
        "lbhts,lbthd->lbshd", weights, grad_blocks, preferred_element_type=jnp.float32
    )
    value_part = value_part + jnp.where(
        seen_bwd,
        jnp.einsum(
            "lbshd,lbhde->lbshe", key_blocks, bwd_states, preferred_element_type=jnp.float32
        ),
        0.0,
    )
    out_shape = (layer_count, row_count, channels)
    query_grad = query_part.reshape(out_shape).astype(jnp.bfloat16)
    key_grad = key_part.reshape(out_shape).astype(jnp.bfloat16)
    value_grad = value_part.reshape(out_shape).astype(jnp.bfloat16)
    return (query_grad, key_grad, value_grad, gain_grad)


def solution(mesh):
    in_specs = (
        P(None, "seq", "fsdp"),
        P(None, "seq", "fsdp"),
        P(None, "seq", "fsdp"),
        P(None, "seq", "fsdp"),
        P(None, "fsdp"),
        P(),
        P("seq"),
    )
    out_specs = (
        P(None, "seq", "fsdp"),
        P(None, "seq", "fsdp"),
        P(None, "seq", "fsdp"),
        P(None, "fsdp"),
    )
    return jax.shard_map(local, mesh=mesh, in_specs=in_specs, out_specs=out_specs, check_vma=False)
```

profile of v0, /device:TPU:1, one launch (start us, length us, event | category | flops | bytes accessed | tf_op | source)
XLA Modules:
  0.0 440.9 jit_solution(18146484628150927812)
XLA Ops:
  11.4 2.4 reshape.141
  13.7 2.8 reshape.142
  16.5 3.1 copy.97
  19.6 2.0 fusion.13
  26.6 2.4 reshape.140
  29.0 3.1 copy.112
  33.5 28.8 %all-reduce = f32[16]{0:T(128)} all-reduce(f32[16]{0:T(128)S(1)} %dynamic-update-slice), channel_id=1, replica_groups=mesh['seq'=16,'fsdp'=16] {'seq'}, use_global_device_ids=true, to_apply=%add | all-reduce | flops 16 | bytes 128
  63.7 2.0 select_convert_fusion.1
  65.7 2.7 copy-done.2
  68.3 3.8 fusion.20
  72.2 1.9 all-gather.3.cloned.1.call-done
  74.1 57.7 %while.34 = (s32[]{:T(128)}, f32[]{:T(128)}, f32[3,2,128,128]{3,2,1,0:T(8,128)S(1)}, s32[]{:T(128)}, f32[16]{0:T(128)S(1)}, /*index=5*/f32[16,3,2,128,128]{4,3,2,1,0:T(8,128)}, s32[]{:T(128)}, f32[]{:T(128)}, s32[]{:T(128)}) while((s32[]{:T(128)}, f32[]{:T(128)}, f32[3,2,128,128]{3,2,1,0:T(8,128)S(1)}, s32[]{:T(128)}, ...), condition=%wide.region_1.2_spmd.clone, body=%wide.region_0.1_spmd.clone.sunk | while | flops 393225 | bytes 1179833 | solution.py:29
  76.5 1.1 fusion.55
  80.1 1.1 fusion.55
  94.6 1.1 fusion.55
  98.2 1.1 fusion.55
  101.8 1.1 fusion.55
  116.2 1.1 fusion.55
  119.8 1.1 fusion.55
  123.4 1.1 fusion.55
  127.0 1.1 fusion.55
  132.1 4.3 multiply_reduce_fusion
  136.4 60.6 %psum.21 = f32[3,1024]{1,0:T(4,128)S(1)} all-reduce(f32[3,1024]{1,0:T(4,128)S(1)} %bitcast.78), channel_id=1, replica_groups=mesh['seq'=16,'fsdp'=16] {'fsdp'}, use_global_device_ids=true, to_apply=%region_3.4 | all-reduce | flops 3072 | bytes 24576 | tf_op jit(solution)/shard_map/psum | solution.py:103
  197.0 5.8 %copy.101 = f32[3,2,512,2,128]{4,3,2,1,0:T(2,128)} copy(f32[3,2,512,2,128]{2,4,3,1,0:T(8,128)} %get-tuple-element.356) | data formatting | bytes 6291456 | tf_op jit(solution)/shard_map/add | solution.py:96
  202.8 4.2 reshape.143
  206.9 2.7 fusion.8
  209.6 55.6 %psum.22 = f32[3,1024]{1,0:T(4,128)S(1)} all-reduce(f32[3,1024]{1,0:T(4,128)S(1)} %get-tuple-element.316), channel_id=1, replica_groups=mesh['seq'=16,'fsdp'=16] {'fsdp'}, use_global_device_ids=true, to_apply=%region_5.6 | all-reduce | flops 3072 | bytes 24576 | tf_op jit(solution)/shard_map/psum | solution.py:106
  265.2 3.0 fusion.6
  268.2 2.5 reshape.144
  275.1 5.1 %copy.117 = bf16[3,2,512,2,128]{2,4,3,1,0:T(8,128)(2,1)} copy(bf16[3,2,512,2,128]{4,3,2,1,0:T(2,128)(2,1)} %copy-done.12) | data formatting | bytes 3145728 | tf_op jit(solution)/shard_map/reshape | solution.py:113
  280.2 3.6 select_convert_fusion
  283.9 2.2 fusion.25
  287.4 2.9 copy.108
  290.3 3.9 convert_element_type.48
  294.2 54.7 %all-reduce.2 = (f32[16]{0:T(128)S(1)}, f32[3,256]{1,0:T(4,128)}) all-reduce(f32[16]{0:T(128)S(1)} %dynamic-update-slice.1, f32[3,256]{1,0:T(4,128)S(1)} %broadcast_multiply_fusion), channel_id=1, replica_groups=mesh['seq'=16,'fsdp'=16] {'seq'}, use_global_device_ids=true, to_apply=%add.1 | all-reduce | flops 784 | bytes 6272
  349.0 6.1 %fusion.45 = f32[3,2,2,128,512]{4,3,2,1,0:T(8,128)} fusion(bf16[3,2,512,2,128]{2,4,3,1,0:T(8,128)(2,1)} %copy.117, bf16[3,2,2,512,512]{4,3,2,1,0:T(8,128)(2,1)} %copy-done.2), kind=kOutput, calls=%fused_computation.78 | convolution fusion | flops 805306368 | bytes 11010048 | tf_op jit(solution)/shard_map/lbhts,lbthd->lbshd/dot_general | solution.py:150
  355.1 2.9 fusion.28
  358.0 59.2 %while.35 = (s32[]{:T(128)}, f32[]{:T(128)}, f32[3,2,128,128]{3,2,1,0:T(8,128)S(1)}, s32[]{:T(128)}, f32[16]{0:T(128)S(1)}, /*index=5*/f32[16,3,2,128,128]{4,3,2...) while((s32[]{:T(128)}, f32[]{:T(128)}, ...), condition=%wide.region_7.8_spmd.clone, body=%wide.region_6.7_spmd.clone.sunk | while | flops 393229 | bytes 1179895 | solution.py:29
  360.5 1.1 fusion.56
  364.2 1.1 fusion.56
  367.9 1.1 fusion.56
  382.7 1.1 fusion.56
  418.5 3.7 fusion.19
  422.2 3.6 copy.120
  425.8 2.3 convert_element_type.53
  428.1 2.5 fusion.9
  430.5 1.2 copy.116
  431.7 2.3 convert_element_type.50
  (143 shorter events, 53.4 us)
Async XLA Ops:
  7.2 66.9 %all-gather.3.cloned.1.call-start = ((), (), s32[]{:S(2)}) async-start(), calls=%async_computation | async-start | bytes 6684672 | tf_op jit(solution)/shard_map/all_gather | solution.py:16
  13.7 49.2 %copy-start.4 = (bf16[3,2,512,2,128]{4,3,2,1,0:T(2,128)(2,1)}, bf16[3,2,512,2,128]{4,3,2,1,0:T(2,128)(2,1)S(1)}, u32[]{:S(2)}) copy-start(bf16[3,2,512,2,128]{4,3,2,1,0:T(2,128)(2,1)S(1)} %reshape.141) | copy-start | bytes 4718596
  16.5 3.1 copy-start.7
  21.6 0.9 copy-start.18
  23.3 334.6 %all-gather.5.cloned.1.call-start = ((), (), s32[]{:S(2)}) async-start(), calls=%async_computation.1 | async-start | bytes 6684672 | tf_op jit(solution)/shard_map/all_gather | solution.py:16
  29.0 103.1 %copy-start = (bf16[3,2,512,2,128]{4,3,2,1,0:T(2,128)(2,1)}, bf16[3,2,512,2,128]{4,3,2,1,0:T(2,128)(2,1)S(1)}, u32[]{:S(2)}) copy-start(bf16[3,2,512,2,128]{4,3,2,1,0:T(2,128)(2,1)S(1)} %reshape.140) | copy-start | bytes 4718596
  29.0 3.1 copy-start.25
  29.0 33.4 %copy-start.24 = (s32[3]{0:T(128)S(1)}, s32[3]{0:T(128)}, u32[]{:S(2)}) copy-start(s32[3]{0:T(128)} %param.16) | copy-start | bytes 40
  62.9 0.8 copy-start.21
  63.7 4.6 %copy-start.8 = (bf16[3,2,512,2,128]{4,3,2,1,0:T(2,128)(2,1)S(1)}, bf16[3,2,512,2,128]{4,3,2,1,0:T(2,128)(2,1)}, u32[]{:S(2)}) copy-start(bf16[3,2,512,2,128]{4,3,2,1,0:T(2,128)(2,1)} %copy-done.7) | copy-start | bytes 4718596
  65.7 2.7 copy-start.2
  68.3 5.8 %copy-start.26 = (f32[16]{0:T(128)S(1)}, f32[16]{0:T(128)}, u32[]{:S(2)}) copy-start(f32[16]{0:T(128)} %all-reduce) | copy-start | bytes 196
  74.1 57.7 %copy-start.19 = (f32[2,3,2,128,128]{4,3,2,1,0:T(8,128)S(1)}, f32[2,3,2,128,128]{4,3,2,1,0:T(8,128)}, u32[]{:S(2)}) copy-start(f32[2,3,2,128,128]{4,3,2,1,0:T(8,128)} %copy-done.18) | copy-start | bytes 2359300
  131.9 4.5 %copy-start.13 = (bf16[3,1,2,128,128]{4,3,2,0,1:T(8,128)(2,1)}, bf16[3,1,2,128,128]{4,3,2,0,1:T(8,128)(2,1)S(1)}, u32[]{:S(2)}) copy-start(bf16[3,1,2,128,128]{4,3,2,0,1:T(8,128)(2,1)S(1)} %get-tuple-element.347) | copy-start | bytes 589828
  131.9 4.5 %copy-start.15 = (bf16[3,1,2,128,128]{4,3,2,0,1:T(8,128)(2,1)}, bf16[3,1,2,128,128]{4,3,2,0,1:T(8,128)(2,1)S(1)}, u32[]{:S(2)}) copy-start(bf16[3,1,2,128,128]{4,3,2,0,1:T(8,128)(2,1)S(1)} %get-tuple-element.348) | copy-start | bytes 589828
  202.8 4.2 copy-start.23
  268.2 2.5 copy-start.20
  270.7 1.1 copy-start.12
  271.9 0.9 copy-start.17
  275.1 5.1 %copy-start.9 = (bf16[3,2,512,2,128]{4,3,2,1,0:T(2,128)(2,1)S(1)}, bf16[3,2,512,2,128]{4,3,2,1,0:T(2,128)(2,1)}, u32[]{:S(2)}) copy-start(bf16[3,2,512,2,128]{4,3,2,1,0:T(2,128)(2,1)} %copy-done.7) | copy-start | bytes 4718596
  275.1 5.1 %copy-start.22 = (pred[2,512,512]{2,1,0:T(8,128)(4,1)S(1)}, pred[2,512,512]{2,1,0:T(8,128)(4,1)}, u32[]{:S(2)}) copy-start(pred[2,512,512]{2,1,0:T(8,128)(4,1)} %copy-done.21) | copy-start | bytes 1572868
  280.2 3.6 copy-start.5
  283.9 2.8 copy-start.3
  283.9 2.8 copy-start.11
  283.9 2.8 copy-start.14
  283.9 2.9 copy-start.16
  290.3 64.8 %slice-start = ((s8[6291456]{0:T(1024)(128)(4,1)}), s8[2097152]{0:T(1024)(128)(4,1)S(1)}, s32[]{:S(2)}) async-start(s8[6291456]{0:T(1024)(128)(4,1)} %bitcast.76), calls=%async_computation.2 | async-start | bytes 4194304
  349.0 6.1 %copy-start.1 = (bf16[3,2,512,2,128]{4,3,2,1,0:T(2,128)(2,1)S(1)}, bf16[3,2,512,2,128]{4,3,2,1,0:T(2,128)(2,1)}, u32[]{:S(2)}) copy-start(bf16[3,2,512,2,128]{4,3,2,1,0:T(2,128)(2,1)} %copy-done) | copy-start | bytes 4718596
  349.0 6.1 %slice-start.1 = ((s8[6291456]{0:T(1024)(128)(4,1)}), s8[4194304]{0:T(1024)(128)(4,1)S(1)}, s32[]{:S(2)}) async-start(s8[6291456]{0:T(1024)(128)(4,1)} %bitcast.76), calls=%async_computation.3 | async-start | bytes 8388608
  358.0 60.5 %copy-start.6 = (bf16[3,2,512,2,128]{4,3,2,1,0:T(2,128)(2,1)S(1)}, bf16[3,2,512,2,128]{4,3,2,1,0:T(2,128)(2,1)}, u32[]{:S(2)}) copy-start(bf16[3,2,512,2,128]{4,3,2,1,0:T(2,128)(2,1)} %copy-done.4) | copy-start | bytes 4718596
  425.8 2.3 copy-start.10
Sparse Core Ops, SparseCore 0:
  23.5 50.5 all-gather.2
  273.7 68.2 all-gather.4
where the time goes:
time: 444 us; the launch traced here: 441 us
  blocking collectives  200 us (45%)
  local copies, waits for them, and re-layouts  76 us (17%)
  loops' own time  61.4 us (14%)
  other arithmetic  46.4 us (10%)
  matrix products  34.2 us (8%)
  between operations  21 us (5%)
    unnamed x2, blocking collectives  83.6 us
    another operation x2, loops' own time, entering(): return lax.fori_loop(0, count, step, start)  61.4 us
    psum x1, blocking collectives, local(): total_squares = lax.psum(local_squares, 'fsdp')  60.6 us
    psum x1, blocking collectives, local(): cross = lax.psum(jnp.sum(weighted * normed, -1), 'fsdp')  55.6 us
    select_n x32, other arithmetic, step(): return jax.tree.map(lambda a, b: jnp.where(reached, a, b), new, before)  36.3 us
    dynamic_slice x32, local copies, waits for them, and re-layouts, step(): new = combine(before, jax.tree.map(lambda part: part[at], everything))  19.2 us
  transfers between devices with their start and end apart: 2, of which 1 were waited for; matrix products, arithmetic and copies ran while one was open for 9% of the time, Pallas kernels for 0%

commit v1 on v0

v1 whole, which is shorter than its diff:
```python
import functools

import jax
import jax.numpy as jnp
from jax import lax
from jax.experimental import pallas as pl
from jax.experimental.pallas import tpu as pltpu
from jax.sharding import PartitionSpec as P

DH = 128
BLK = 256
EPSILON = 1e-06
KEEP_RATE = 0.75
F32 = jnp.float32
BF16 = jnp.bfloat16
MESH = pl.DeviceIdType.MESH


def dot(a, b, ca, cb):
    return lax.dot_general(a, b, (((ca,), (cb,)), ((), ())), preferred_element_type=F32)


def same(a, b):
    return jnp.where(a == b, 1.0, 0.0).astype(F32)


def kernel(
    nz, nf, layers, rows, heads,
    q_hbm, k_hbm, v_hbm, g_hbm, gain_ref, keep_ref, seg_ref,
    dq_ref, dk_ref, dv_ref, gg_ref,
    q_ref, k_ref, v_ref, g_ref, ld_sem,
    segrow, segcol, mask, maskt, mytile, ptile, tabz,
    tails, fronts, cq, qs, qmt, ks, vs, pt, o_ref, do_ref, kpart, vpart,
    dsum, dpart, tot, slots, ebuf, ein, xbuf, dev,
    stat, gtile, gptile, gsum, gslots,
    tile_s, tile_r, tab_s, tab_r,
    d_s, d_r, a_s, a_r, e_s, e_r, x_s, x_r,
    st_s, st_r, gt_s, gt_r, gz_s, gz_r,
):
    nb = rows // BLK
    cut = DH // nz
    features = heads * DH * nf
    s = lax.axis_index("seq")
    f = lax.axis_index("fsdp")
    z = s // 2
    c = s % 2
    partner = (2 * z + 1 - c, f)
    pending = []

    def zmod(x):
        return lax.rem(x + 2 * nz, nz)

    def zpeer(j):
        return (2 * zmod(z + j) + c, f)

    def fpeer(j):
        return (s, lax.rem(f + j, nf))

    def send(src, dst, ss, rs, to):
        copy = pltpu.make_async_remote_copy(
            src_ref=src, dst_ref=dst, send_sem=ss, recv_sem=rs, device_id=to, device_id_type=MESH
        )
        copy.start()
        pending.append(copy)

    def arrived(src, dst, ss, rs, to):
        pltpu.make_async_remote_copy(
            src_ref=src, dst_ref=dst, send_sem=ss, recv_sem=rs, device_id=to, device_id_type=MESH
        ).wait_recv()

    def flush():
        for copy in pending:
            copy.wait_send()
        pending.clear()

    def load(i, hbm, ref, l):
        return pltpu.make_async_copy(hbm.at[l], ref.at[l], ld_sem.at[i, l])

    for l in range(layers):
        load(0, k_hbm, k_ref, l).start()
        load(1, v_hbm, v_ref, l).start()
    for l in range(layers):
        load(2, q_hbm, q_ref, l).start()
    for l in range(layers):
        load(3, g_hbm, g_ref, l).start()

    barrier = pltpu.get_barrier_semaphore()
    pl.semaphore_signal(barrier, inc=1, device_id=partner, device_id_type=MESH)
    for j in range(1, nz):
        pl.semaphore_signal(barrier, inc=1, device_id=zpeer(j), device_id_type=MESH)
    for j in range(1, nf):
        pl.semaphore_signal(barrier, inc=1, device_id=fpeer(j), device_id_type=MESH)

    seg = seg_ref[...].astype(F32)
    for i in range(rows // 128):
        segrow[0:1, 128 * i : 128 * (i + 1)] = seg[i : i + 1, :]
        segcol[128 * i : 128 * (i + 1), :] = jnp.broadcast_to(seg[i : i + 1, :], (128, 128)).T
    first = [segcol[BLK * b : BLK * b + 1, :] for b in range(nb)]
    last = [segcol[BLK * b + BLK - 1 : BLK * b + BLK, :] for b in range(nb)]
    tile_row = lax.broadcasted_iota(jnp.int32, (8, 128), 0)
    mytile[...] = jnp.where(
        tile_row == 2 * c, first[0], jnp.where(tile_row == 2 * c + 1, last[nb - 1], 0.0)
    )

    def blk(b):
        return slice(BLK * b, BLK * (b + 1))

    def hd(h):
        return slice(DH * h, DH * (h + 1))

    def column_mask(b, value):
        return same(segcol[blk(b), :], value).astype(BF16)

    def hand_over(w, l):
        send(dsum.at[w, l, 1 - c], dpart.at[w, l], d_s.at[w, l], d_r.at[w, l], partner)

    def chip_total(w, l, own_weight, partner_weight):
        arrived(dsum.at[w, l, 1 - c], dpart.at[w, l], d_s.at[w, l], d_r.at[w, l], partner)
        total = own_weight * dsum[w, l, c] + partner_weight * dpart[w, l]
        tot[w, l] = total
        for j in range(1, nz):
            at = pl.multiple_of(zmod(z + j) * cut, cut)
            send(
                tot.at[w, l, pl.ds(at, cut)], slots.at[w, l, z],
                a_s.at[w, l, j - 1], a_r.at[w, l, j - 1], zpeer(j),
            )
        slots[w, l, z] = tot[w, l, pl.ds(pl.multiple_of(z * cut, cut), cut)]

    def owner(w, l):
        for j in range(1, nz):
            arrived(
                tot.at[w, l, pl.ds(0, cut)], slots.at[w, l, zmod(z - j)],
                a_s.at[w, l, j - 1], a_r.at[w, l, j - 1], zpeer(j),
            )
        if w == 0:
            edge = [tabz[i, 3:4, :] for i in range(nz)]
            order = list(range(nz))
        else:
            edge = [tabz[i, 0:1, :] for i in range(nz)]
            order = list(range(nz))[::-1]
        state = jnp.zeros((cut, DH), F32)
        for n, i in enumerate(order):
            if n == 1:
                state = slots[w, l, order[0]]
            elif n > 1:
                state = slots[w, l, order[n - 1]] + same(edge[order[n - 2]], edge[order[n - 1]]) * state
            ebuf[w, l, i] = state
        for j in range(1, nz):
            send(
                ebuf.at[w, l, zmod(z + j)],
                ein.at[w, l, pl.ds(pl.multiple_of(z * cut, cut), cut)],
                e_s.at[w, l, j - 1], e_r.at[w, l, j - 1], zpeer(j),
            )
        ein[w, l, pl.ds(pl.multiple_of(z * cut, cut), cut)] = ebuf[w, l, z]

    def entering(w, l, joined):
        for j in range(1, nz):
            at = pl.multiple_of(zmod(z - j) * cut, cut)
            arrived(
                ebuf.at[w, l, 0], ein.at[w, l, pl.ds(at, cut)],
                e_s.at[w, l, j - 1], e_r.at[w, l, j - 1], zpeer(j),
            )
        state = ein[w, l]
        second = c == 1 - w
        own_weight = jnp.where(second, joined, 1.0)
        partner_weight = jnp.where(second, 1.0, joined)
        zero = jnp.zeros((1, DH), F32)
        own_add = jnp.where(second, zero + 1.0, zero)
        partner_add = jnp.where(second, zero, zero + 1.0)
        xbuf[w, l] = partner_weight * state + partner_add * dsum[w, l, c]
        send(xbuf.at[w, l], dev.at[w, l, c], x_s.at[w, l], x_r.at[w, l], partner)
        dev[w, l, c] = own_weight * state + own_add * dpart[w, l]

    def entered(w, l):
        arrived(xbuf.at[w, l], dev.at[w, l, 1 - c], x_s.at[w, l], x_r.at[w, l], partner)

    tail_masks = [column_mask(b, last[b]) for b in range(nb)]
    for l in range(layers):
        load(0, k_hbm, k_ref, l).wait()
        load(1, v_hbm, v_ref, l).wait()
        for h in range(heads):
            total = None
            for b in range(nb):
                part = dot(k_ref[l, blk(b), hd(h)], v_ref[l, blk(b), hd(h)] * tail_masks[b], 0, 0)
                tails[l, h, b] = part
                part = part * same(last[b], last[nb - 1])
                total = part if total is None else total + part
            dsum[0, l, h] = total
        if l == 0:
            pl.semaphore_wait(barrier, 1 + (nz - 1) + (nf - 1))
            send(mytile, ptile, tile_s, tile_r, partner)
        hand_over(0, l)

    arrived(mytile, ptile, tile_s, tile_r, partner)
    chiptile = mytile[...] + ptile[...]
    tabz[z] = chiptile
    for j in range(1, nz):
        send(tabz.at[z], tabz.at[z], tab_s.at[j - 1], tab_r.at[j - 1], zpeer(j))
    first0, last0 = chiptile[0:1], chiptile[1:2]
    first1, last1 = chiptile[2:3], chiptile[3:4]
    is0 = c == 0
    end_own = jnp.where(is0, same(last0, last1), 1.0)
    end_partner = jnp.where(is0, 1.0, same(last0, last1))
    begin_own = jnp.where(is0, 1.0, same(first0, first1))
    begin_partner = jnp.where(is0, same(first0, first1), 1.0)
    for l in range(layers):
        chip_total(0, l, end_own, end_partner)

    at_t = lax.broadcasted_iota(jnp.int32, (BLK, BLK), 0)
    at_s = lax.broadcasted_iota(jnp.int32, (BLK, BLK), 1)
    for b in range(nb):
        wide = jnp.concatenate([segcol[blk(b), :]] * (BLK // 128), axis=1)
        equal = wide == segrow[0:1, blk(b)]
        mask[b] = jnp.where(jnp.logical_and(equal, at_t >= at_s), 1.0, 0.0).astype(BF16)
        maskt[b] = jnp.where(jnp.logical_and(equal, at_s >= at_t), 1.0, 0.0).astype(BF16)

    for l in range(layers):
        load(2, q_hbm, q_ref, l).wait()

    def inner(l, carry):
        for h in range(heads):
            for b in range(nb):
                scores = dot(q_ref[l, blk(b), hd(h)], k_ref[l, blk(b), hd(h)], 1, 1)
                weights = scores.astype(BF16) * mask[b]
                o_ref[l, blk(b), hd(h)] = dot(weights, v_ref[l, blk(b), hd(h)], 1, 0)
        return carry

    lax.fori_loop(0, layers, inner, 0)

    for j in range(1, nz):
        arrived(tabz.at[z], tabz.at[zmod(z - j)], tab_s.at[j - 1], tab_r.at[j - 1], zpeer(j))
    for l in range(layers):
        owner(0, l)

    before_chip = tabz[zmod(z - 1), 3:4, :]
    after_chip = tabz[zmod(z + 1), 0:1, :]
    before = jnp.where(is0, before_chip, last0)
    after = jnp.where(is0, first1, after_chip)
    prior = [before] + last[: nb - 1]
    later = first[1:] + [after]

    def prepare(l, carry):
        for b in range(nb):
            seen_f = column_mask(b, prior[b])
            seen_b = column_mask(b, later[b])
            head = column_mask(b, first[b])
            for h in range(heads):
                q = q_ref[l, blk(b), hd(h)]
                k = k_ref[l, blk(b), hd(h)]
                qs[l, blk(b), hd(h)] = q * seen_f
                qmt[l, hd(h), blk(b)] = (q * head).T
                ks[l, blk(b), hd(h)] = k * seen_b
                vs[l, blk(b), hd(h)] = v_ref[l, blk(b), hd(h)] * seen_b
                pt[l, h, b] = dot(k, q, 1, 1).astype(BF16) * maskt[b]
        return carry

    lax.fori_loop(0, layers, prepare, 0)

    for l in range(layers):
        load(3, g_hbm, g_ref, l).wait()
    joined = same(before_chip, last0)
    for l in range(layers):
        entering(0, l, joined)

    ones = jnp.ones((8, DH), BF16)

    def sums(x):
        high = x.astype(BF16)
        low = (x - high.astype(F32)).astype(BF16)
        total = dot(ones, high, 1, 1) + dot(ones, low, 1, 1)
        tile = jnp.zeros((8, 128), F32)
        for i in range(rows // 128):
            tile = jnp.where(tile_row == i, total[:, 128 * i : 128 * (i + 1)], tile)
        return tile

    for l in range(layers):
        entered(0, l)
        for h in range(heads):
            state = dev[0, l, h]
            for b in range(nb):
                if b:
                    state = tails[l, h, b - 1] + same(prior[b - 1], prior[b]) * state
                cq[l, h, b] = state.astype(BF16)
        squares, crosses = [], []
        for b in range(nb):
            square, cross = None, None
            for h in range(heads):
                o = o_ref[l, blk(b), hd(h)] + dot(qs[l, blk(b), hd(h)], cq[l, h, b], 1, 0)
                o_ref[l, blk(b), hd(h)] = o
                a = g_ref[l, blk(b), hd(h)].astype(F32) * gain_ref[l : l + 1, hd(h)]
                square = o * o if square is None else square + o * o
                cross = a * o if cross is None else cross + a * o
            squares.append(square)
            crosses.append(cross)
        stat[l, f, 0:8, :] = sums(jnp.concatenate(squares, axis=0))
        stat[l, f, 8:16, :] = sums(jnp.concatenate(crosses, axis=0))
        for j in range(1, nf):
            send(stat.at[l, f], stat.at[l, f], st_s.at[l, j - 1], st_r.at[l, j - 1], fpeer(j))

    for l in range(layers):
        for j in range(1, nf):
            arrived(
                stat.at[l, f], stat.at[l, lax.rem(f + nf - j, nf)],
                st_s.at[l, j - 1], st_r.at[l, j - 1], fpeer(j),
            )
        both = stat[l, 0]
        for i in range(1, nf):
            both = both + stat[l, i]
        r = lax.rsqrt(both[0:8] / features + EPSILON)
        keep = keep_ref[l].astype(F32) / KEEP_RATE
        scale_a = keep * r
        scale_o = scale_a * (r * r) * (both[8:16] / features)
        turned = jnp.concatenate([scale_a, scale_o, jnp.zeros((112, 128), F32)], axis=0).T
        gains = [jnp.zeros((1, DH), F32) for h in range(heads)]
        totals = [None] * heads
        for b in range(nb):
            per = BLK // 128
            col_a = jnp.concatenate(
                [jnp.broadcast_to(turned[:, per * b + i : per * b + i + 1], (128, 128)) for i in range(per)], axis=0
            )
            col_o = jnp.concatenate(
                [jnp.broadcast_to(turned[:, 8 + per * b + i : 9 + per * b + i], (128, 128)) for i in range(per)], axis=0
            )
            for h in range(heads):
                o = o_ref[l, blk(b), hd(h)]
                up = g_ref[l, blk(b), hd(h)].astype(F32) * col_a
                gains[h] = gains[h] + jnp.sum(up * o, axis=0, keepdims=True)
                grad = (up * gain_ref[l : l + 1, hd(h)] - o * col_o).astype(BF16)
                do_ref[l, blk(b), hd(h)] = grad
                part = dot(qmt[l, hd(h), blk(b)], grad, 1, 0)
                fronts[l, h, b] = part
                part = part * same(first[b], first[0])
                totals[h] = part if totals[h] is None else totals[h] + part
        for h in range(heads):
            dsum[1, l, h] = totals[h]
            gtile[heads * l + h : heads * l + h + 1, :] = gains[h]
        hand_over(1, l)
    for i in range(heads * layers, 8):
        gtile[i : i + 1, :] = jnp.zeros((1, DH), F32)
    send(gtile, gptile, gt_s, gt_r, partner)
    for l in range(layers):
        chip_total(1, l, begin_own, begin_partner)

    def outer(l, carry):
        for h in range(heads):
            for b in range(nb):
                grad = do_ref[l, blk(b), hd(h)]
                v = v_ref[l, blk(b), hd(h)]
                vpart[l, blk(b), hd(h)] = dot(pt[l, h, b], grad, 1, 0)
                gst = dot(v, grad, 1, 1).astype(BF16) * maskt[b]
                kpart[l, blk(b), hd(h)] = dot(gst, q_ref[l, blk(b), hd(h)], 1, 0)
        return carry

    lax.fori_loop(0, layers, outer, 0)
    arrived(gtile, gptile, gt_s, gt_r, partner)
    gslots[z] = gtile[...] + gptile[...]
    for j in range(1, nz):
        send(gslots.at[z], gslots.at[z], gz_s.at[j - 1], gz_r.at[j - 1], zpeer(j))
    for l in range(layers):
        owner(1, l)

    def outer_q(l, carry):
        for h in range(heads):
            for b in range(nb):
                grad = do_ref[l, blk(b), hd(h)]
                gs = dot(grad, v_ref[l, blk(b), hd(h)], 1, 1).astype(BF16) * mask[b]
                seen_f = column_mask(b, prior[b])
                dq_ref[l, blk(b), hd(h)] = (
                    dot(gs, k_ref[l, blk(b), hd(h)], 1, 0) + dot(grad * seen_f, cq[l, h, b], 1, 1)
                ).astype(BF16)
        return carry

    lax.fori_loop(0, layers, outer_q, 0)
    for j in range(1, nz):
        arrived(gslots.at[z], gslots.at[zmod(z - j)], gz_s.at[j - 1], gz_r.at[j - 1], zpeer(j))
    gtotal = gslots[0]
    for i in range(1, nz):
        gtotal = gtotal + gslots[i]
    for l in range(layers):
        for h in range(heads):
            gg_ref[l : l + 1, hd(h)] = gtotal[heads * l + h : heads * l + h + 1, :]

    joined = same(after_chip, first1)
    for l in range(layers):
        entering(1, l, joined)
    flush()

    for l in range(layers):
        entered(1, l)
        for h in range(heads):
            state = dev[1, l, h]
            for b in range(nb)[::-1]:
                if b < nb - 1:
                    state = fronts[l, h, b + 1] + same(later[b + 1], later[b]) * state
                rq = state.astype(BF16)
                dk_ref[l, blk(b), hd(h)] = (
                    kpart[l, blk(b), hd(h)] + dot(vs[l, blk(b), hd(h)], rq, 1, 1)
                ).astype(BF16)
                dv_ref[l, blk(b), hd(h)] = (
                    vpart[l, blk(b), hd(h)] + dot(ks[l, blk(b), hd(h)], rq, 1, 0)
                ).astype(BF16)


def local(queries, keys, values, out_grad, gain, keep_mask, segments):
    layers, rows, channels = queries.shape
    heads = channels // DH
    nz = lax.axis_size("seq") // 2
    nf = lax.axis_size("fsdp")
    nb = rows // BLK
    cut = DH // nz
    whole = (layers, rows, channels)
    vmem = pltpu.VMEM
    dma = pltpu.SemaphoreType.DMA
    hbm = pl.BlockSpec(memory_space=pl.ANY)
    near = pl.BlockSpec(memory_space=pltpu.VMEM)
    scratch = [
        vmem(whole, BF16), vmem(whole, BF16), vmem(whole, BF16), vmem(whole, BF16), dma((4, layers)),
        vmem((1, rows), F32), vmem((rows, 128), F32), vmem((nb, BLK, BLK), BF16), vmem((nb, BLK, BLK), BF16),
        vmem((8, 128), F32), vmem((8, 128), F32), vmem((nz, 8, 128), F32),
        vmem((layers, heads, nb, DH, DH), F32), vmem((layers, heads, nb, DH, DH), F32),
        vmem((layers, heads, nb, DH, DH), BF16),
        vmem(whole, BF16), vmem((layers, channels, rows), BF16), vmem(whole, BF16), vmem(whole, BF16),
        vmem((layers, heads, nb, BLK, BLK), BF16),
        vmem(whole, F32), vmem(whole, BF16), vmem(whole, F32), vmem(whole, F32),
        vmem((2, layers, heads, DH, DH), F32), vmem((2, layers, DH, DH), F32), vmem((2, layers, DH, DH), F32),
        vmem((2, layers, nz, cut, DH), F32), vmem((2, layers, nz, cut, DH), F32),
        vmem((2, layers, DH, DH), F32), vmem((2, layers, DH, DH), F32), vmem((2, layers, heads, DH, DH), F32),
        vmem((layers, nf, 16, 128), F32),
        vmem((8, 128), F32), vmem((8, 128), F32), vmem((8, 128), F32), vmem((nz, 8, 128), F32),
        dma, dma, dma((nz - 1,)), dma((nz - 1,)),
        dma((2, layers)), dma((2, layers)),
        dma((2, layers, nz - 1)), dma((2, layers, nz - 1)),
        dma((2, layers, nz - 1)), dma((2, layers, nz - 1)),
        dma((2, layers)), dma((2, layers)),
        dma((layers, nf - 1)), dma((layers, nf - 1)),
        dma, dma, dma((nz - 1,)), dma((nz - 1,)),
    ]
    return pl.pallas_call(
        functools.partial(kernel, nz, nf, layers, rows, heads),
        out_shape=(
            jax.ShapeDtypeStruct(whole, BF16),
            jax.ShapeDtypeStruct(whole, BF16),
            jax.ShapeDtypeStruct(whole, BF16),
            jax.ShapeDtypeStruct((layers, channels), F32),
        ),
        in_specs=[hbm, hbm, hbm, hbm, near, pl.BlockSpec(memory_space=pltpu.SMEM), near],
        out_specs=(near, near, near, near),
        scratch_shapes=scratch,
        compiler_params=pltpu.CompilerParams(
            collective_id=0, has_side_effects=True, vmem_limit_bytes=56 * 2**20
        ),
        name="backward",
    )(queries, keys, values, out_grad, gain, keep_mask, segments.reshape(rows // 128, 128))


def solution(mesh):
    wide = P(None, "seq", "fsdp")
    in_specs = (wide, wide, wide, wide, P(None, "fsdp"), P(), P("seq"))
    out_specs = (wide, wide, wide, P(None, "fsdp"))
    return jax.shard_map(local, mesh=mesh, in_specs=in_specs, out_specs=out_specs, check_vma=False)
```

time: 444 us -> 63.2 us (0.14)
  blocking collectives: 200 us -> 0 us
  local copies, waits for them, and re-layouts: 76 us -> 6.49 us
  loops' own time: 61.4 us -> 0 us
  Pallas kernels: 0 us -> 55.9 us
  other arithmetic: 46.4 us -> 0 us
  matrix products: 34.2 us -> 0 us
  between operations: 21 us -> 0.65 us
    psum x2 -> x0, blocking collectives: 116 us -> none  [the longest x1 60.6 us: local(): total_squares = lax.psum(local_squares, 'fsdp')]
    unnamed x2 -> x0, blocking collectives: 83.6 us -> none
    another operation x2 -> x0, loops' own time: 61.4 us -> none  [entering(): return lax.fori_loop(0, count, step, start)]
    pallas_call x0 -> x1, Pallas kernels: none -> 55.9 us  [local(): pl.pallas_call(functools.partial(kernel, nz, nf, layers, rows, heads), ou...]
    select_n x32 -> x0, other arithmetic: 36.3 us -> none  [step(): return jax.tree.map(lambda a, b: jnp.where(reached, a, b), new, before)]
    dot_general x12 -> x0, matrix products: 34.2 us -> none  [the longest x1 6.08 us: local(): jnp.einsum('lbhts,lbthd->lbshd', weights, grad_blocks, preferred_element_...]
    reshape x8 -> x0, local copies, waits for them, and re-layouts: 25.4 us -> none  [the longest x2 7.54 us: local(): grad_blocks = d_attention.reshape(shape_blocks)]
    dynamic_slice x32 -> x0, local copies, waits for them, and re-layouts: 19.2 us -> none  [step(): new = combine(before, jax.tree.map(lambda part: part[at], everything))]
  transfers between devices with their start and end apart: 2 -> 0, of which waited for: 1 -> 0; matrix products, arithmetic and copies ran while one was open for 9% -> 0% of each run, Pallas kernels for 0% -> 0%
where the time goes in v1:
time: 63.2 us; the launch traced here: 63.1 us
  Pallas kernels  55.9 us (88%)
  local copies, waits for them, and re-layouts  6.49 us (10%)
  between operations  0.65 us (1%)
    pallas_call x1, Pallas kernels, local(): pl.pallas_call(functools.partial(kernel, nz, nf, layers, rows, heads), ou...  55.9 us
    unnamed x10, local copies, waits for them, and re-layouts  6.49 us

profile of v1, /device:TPU:1, one launch (start us, length us, event | category | flops | bytes accessed | tf_op | source)
XLA Modules:
  0.0 63.1 jit_solution(9234328502369319615)
XLA Ops:
  0.6 55.9 %backward.1 = (bf16[3,1024,256]{2,1,0:T(8,128)(2,1)}, bf16[3,1024,256]{2,1,0:T(8,128)(2,1)}, bf16[3,1024,256]{2,1,0:T(8,128)(2,1)}, f32[3,256]{1,0:T(4,128)}) custom-call(bf16[3,1024,256]{2,1,0:T(8,128)(2,1)} %q_hbm.1, bf16[3,1024,256]{2,1,0:T(8,128)(2,1)} %k_hbm.1, bf16[3,1024,256]{2,1,0:T(8,128)(2,1)} %v_hbm.1, bf16[3,1024,256]{2,1,0:T(8,128)(2,1)} %g_hbm.1, ...), custom_call_target="tpu_custom_call" | custom-call | tf_op jit(solution)/shard_map/backward/pallas_call | solution.py:438
  56.6 0.0 copy-start.1
  56.6 2.8 %copy.15 = bf16[3,1024,256]{2,1,0:T(8,128)(2,1)} copy(bf16[3,1024,256]{2,1,0:T(8,128)(2,1)} %get-tuple-element.8) | data formatting | bytes 3145728
  59.4 0.0 copy-done.1
  59.4 0.0 copy-start
  59.4 1.1 %copy.16 = bf16[3,1024,256]{2,1,0:T(8,128)(2,1)} copy(bf16[3,1024,256]{2,1,0:T(8,128)(2,1)S(1)} %copy-done.1) | data formatting | bytes 3145728
  60.5 0.8 %copy-done = bf16[3,1024,256]{2,1,0:T(8,128)(2,1)S(1)} copy-done((bf16[3,1024,256]{2,1,0:T(8,128)(2,1)S(1)}, bf16[3,1024,256]{2,1,0:T(8,128)(2,1)}, u32[]{:S(2)}) %copy-start) | copy-done | bytes 1572888
  61.3 0.0 copy-start.2
  61.3 1.1 %copy.17 = bf16[3,1024,256]{2,1,0:T(8,128)(2,1)} copy(bf16[3,1024,256]{2,1,0:T(8,128)(2,1)S(1)} %copy-done) | data formatting | bytes 3145728
  62.5 0.0 copy-done.2
  62.5 0.6 copy.18
Async XLA Ops:
  56.6 2.8 %copy-start.1 = (bf16[3,1024,256]{2,1,0:T(8,128)(2,1)S(1)}, bf16[3,1024,256]{2,1,0:T(8,128)(2,1)}, u32[]{:S(2)}) copy-start(bf16[3,1024,256]{2,1,0:T(8,128)(2,1)} %get-tuple-element.9) | copy-start | bytes 4718596
  59.4 2.0 %copy-start = (bf16[3,1024,256]{2,1,0:T(8,128)(2,1)S(1)}, bf16[3,1024,256]{2,1,0:T(8,128)(2,1)}, u32[]{:S(2)}) copy-start(bf16[3,1024,256]{2,1,0:T(8,128)(2,1)} %get-tuple-element.10) | copy-start | bytes 4718596
  61.3 1.1 %copy-start.2 = (f32[3,256]{1,0:T(4,128)S(1)}, f32[3,256]{1,0:T(4,128)}, u32[]{:S(2)}) copy-start(f32[3,256]{1,0:T(4,128)} %get-tuple-element.11) | copy-start | bytes 9220

commit v2 on v1

v2 whole, which is shorter than its diff:
```python
import functools

import jax
import jax.numpy as jnp
from jax import lax
from jax.experimental import pallas as pl
from jax.experimental.pallas import tpu as pltpu
from jax.sharding import PartitionSpec as P

DH = 128
BLK = 256
EPSILON = 1e-06
KEEP_RATE = 0.75
F32 = jnp.float32
BF16 = jnp.bfloat16
MESH = pl.DeviceIdType.MESH


def dot(a, b, ca, cb):
    return lax.dot_general(a, b, (((ca,), (cb,)), ((), ())), preferred_element_type=F32)


def same(a, b):
    return jnp.where(a == b, 1.0, 0.0).astype(F32)


def kernel(
    nz, nf, layers, rows, heads,
    q_hbm, k_hbm, v_hbm, g_hbm, gain_hbm, keep_ref, seg_hbm,
    dq_out, kpart_out, vpart_out, ks_out, vs_out, rq_out, gg_out,
    q_ref, k_ref, v_ref, g_ref, ld_sem, qg_sem, gain_ref, seg_ref, small_sem, out_sem,
    dq_ref, rq_ref, gg_ref,
    segrow, segcol, mask, maskt, mytile, ptile, tabz,
    tails, fronts, cq, qs, qmt, ks, vs, pt, o_ref, do_ref, kpart, vpart,
    dsum, dpart, tot, slots, ebuf, ein, xbuf, dev,
    stat, gtile, gptile, gslots,
    tile_s, tile_r, tab_s, tab_r,
    d_s, d_r, a_s, a_r, e_s, e_r, x_s, x_r,
    st_s, st_r, gt_s, gt_r, gz_s, gz_r,
):
    nb = rows // BLK
    cut = DH // nz
    steps = sorted(range(1, nz), key=lambda j: -min(j, nz - j))
    features = heads * DH * nf
    s = lax.axis_index("seq")
    f = lax.axis_index("fsdp")
    z = s // 2
    c = s % 2
    partner = (2 * z + 1 - c, f)

    def zmod(x):
        return lax.rem(x + 2 * nz, nz)

    def zpeer(j):
        return (2 * zmod(z + j) + c, f)

    def fpeer(j):
        return (s, lax.rem(f + j, nf))

    def remote(src, dst, ss, rs, to):
        return pltpu.make_async_remote_copy(
            src_ref=src, dst_ref=dst, send_sem=ss, recv_sem=rs, device_id=to, device_id_type=MESH
        )

    def sent(part, sem):
        remote(part, part, sem, sem, partner).wait_send()

    def arrived(part, sem):
        remote(part, part, sem, sem, partner).wait_recv()

    def load(i, hbm, ref, l):
        return pltpu.make_async_copy(hbm.at[l], ref.at[l], ld_sem.at[i, l])

    small = (
        pltpu.make_async_copy(seg_hbm, seg_ref, small_sem.at[0]),
        pltpu.make_async_copy(gain_hbm, gain_ref, small_sem.at[1]),
        pltpu.make_async_copy(gg_ref, gg_out, small_sem.at[2]),
    )
    small[0].start()
    load(0, k_hbm, k_ref, 0).start()
    load(1, v_hbm, v_ref, 0).start()
    whole_loads = (
        pltpu.make_async_copy(q_hbm, q_ref, qg_sem.at[0]),
        pltpu.make_async_copy(g_hbm, g_ref, qg_sem.at[1]),
    )

    store_dq, store_k, store_v, store_ks, store_vs, store_rq = (
        pltpu.make_async_copy(ref, out, out_sem.at[i])
        for i, (ref, out) in enumerate((
            (dq_ref, dq_out), (kpart, kpart_out), (vpart, vpart_out),
            (ks, ks_out), (vs, vs_out), (rq_ref, rq_out),
        ))
    )

    barrier = pltpu.get_barrier_semaphore()
    pl.semaphore_signal(barrier, inc=1, device_id=partner, device_id_type=MESH)
    for j in range(1, nz):
        pl.semaphore_signal(barrier, inc=1, device_id=zpeer(j), device_id_type=MESH)
    for j in range(1, nf):
        pl.semaphore_signal(barrier, inc=1, device_id=fpeer(j), device_id_type=MESH)

    small[0].wait()
    for l in range(1, layers):
        load(0, k_hbm, k_ref, l).start()
        load(1, v_hbm, v_ref, l).start()
    seg = seg_ref[...].astype(F32)
    for i in range(rows // 128):
        segrow[0:1, 128 * i : 128 * (i + 1)] = seg[i : i + 1, :]
        segcol[128 * i : 128 * (i + 1), :] = jnp.broadcast_to(seg[i : i + 1, :], (128, 128)).T
    first = [segcol[BLK * b : BLK * b + 1, :] for b in range(nb)]
    last = [segcol[BLK * b + BLK - 1 : BLK * b + BLK, :] for b in range(nb)]
    tile_row = lax.broadcasted_iota(jnp.int32, (8, 128), 0)
    mytile[...] = jnp.where(
        tile_row == 2 * c, first[0], jnp.where(tile_row == 2 * c + 1, last[nb - 1], 0.0)
    )

    def blk(b):
        return slice(BLK * b, BLK * (b + 1))

    def hd(h):
        return slice(DH * h, DH * (h + 1))

    def column_mask(b, value):
        return same(segcol[blk(b), :], value).astype(BF16)

    def hand_over(w, l):
        remote(dsum.at[w, l, 1 - c], dpart.at[w, l], d_s.at[w], d_r.at[w, l], partner).start()

    def chip_total(w, l, own_weight, partner_weight):
        arrived(dpart.at[w, l], d_r.at[w, l])
        total = own_weight * dsum[w, l, c] + partner_weight * dpart[w, l]
        tot[w, l] = total
        for j in steps:
            at = pl.multiple_of(zmod(z + j) * cut, cut)
            remote(
                tot.at[w, l, pl.ds(at, cut)], slots.at[w, l, z], a_s.at[w], a_r.at[w, l], zpeer(j)
            ).start()
        slots[w, l, z] = tot[w, l, pl.ds(pl.multiple_of(z * cut, cut), cut)]

    def owner(w, l):
        arrived(slots.at[w, l, 0 : nz - 1], a_r.at[w, l])
        if w == 0:
            edge = [tabz[i, 3:4, :] for i in range(nz)]
            order = list(range(nz))
        else:
            edge = [tabz[i, 0:1, :] for i in range(nz)]
            order = list(range(nz))[::-1]
        state = jnp.zeros((cut, DH), F32)
        for n, i in enumerate(order):
            if n == 1:
                state = slots[w, l, order[0]]
            elif n > 1:
                state = slots[w, l, order[n - 1]] + same(edge[order[n - 2]], edge[order[n - 1]]) * state
            ebuf[w, l, i] = state
        for j in steps:
            remote(
                ebuf.at[w, l, zmod(z + j)],
                ein.at[w, l, pl.ds(pl.multiple_of(z * cut, cut), cut)],
                e_s.at[w], e_r.at[w, l], zpeer(j),
            ).start()
        ein[w, l, pl.ds(pl.multiple_of(z * cut, cut), cut)] = ebuf[w, l, z]

    def entering(w, l, joined):
        arrived(ein.at[w, l, 0 : DH - cut], e_r.at[w, l])
        state = ein[w, l]
        second = c == 1 - w
        own_weight = jnp.where(second, joined, 1.0)
        partner_weight = jnp.where(second, 1.0, joined)
        zero = jnp.zeros((1, DH), F32)
        own_add = jnp.where(second, zero + 1.0, zero)
        partner_add = jnp.where(second, zero, zero + 1.0)
        xbuf[w, l] = partner_weight * state + partner_add * dsum[w, l, c]
        remote(xbuf.at[w, l], dev.at[w, l, c], x_s.at[w], x_r.at[w, l], partner).start()
        dev[w, l, c] = own_weight * state + own_add * dpart[w, l]

    def entered(w, l):
        arrived(dev.at[w, l, 1 - c], x_r.at[w, l])

    def sent_state(w):
        sent(dsum.at[w, :, 0], d_s.at[w])
        sent(tot.at[w, :, 0 : DH - cut], a_s.at[w])
        sent(ebuf.at[w, :, 0 : nz - 1], e_s.at[w])
        sent(xbuf.at[w], x_s.at[w])

    tail_masks = [column_mask(b, last[b]) for b in range(nb)]
    for l in range(layers):
        load(0, k_hbm, k_ref, l).wait()
        load(1, v_hbm, v_ref, l).wait()
        for h in range(heads):
            total = None
            for b in range(nb):
                part = dot(k_ref[l, blk(b), hd(h)], v_ref[l, blk(b), hd(h)] * tail_masks[b], 0, 0)
                tails[l, h, b] = part
                part = part * same(last[b], last[nb - 1])
                total = part if total is None else total + part
            dsum[0, l, h] = total
    pl.semaphore_wait(barrier, 1 + (nz - 1) + (nf - 1))
    remote(mytile, ptile, tile_s, tile_r, partner).start()
    for l in range(layers):
        hand_over(0, l)
    for copy in whole_loads:
        copy.start()
    small[1].start()

    arrived(ptile, tile_r)
    chiptile = mytile[...] + ptile[...]
    tabz[z] = chiptile
    for j in steps:
        remote(tabz.at[z], tabz.at[z], tab_s, tab_r, zpeer(j)).start()
    first0, last0 = chiptile[0:1], chiptile[1:2]
    first1, last1 = chiptile[2:3], chiptile[3:4]
    is0 = c == 0
    end_own = jnp.where(is0, same(last0, last1), 1.0)
    end_partner = jnp.where(is0, 1.0, same(last0, last1))
    begin_own = jnp.where(is0, 1.0, same(first0, first1))
    begin_partner = jnp.where(is0, same(first0, first1), 1.0)
    for l in range(layers):
        chip_total(0, l, end_own, end_partner)

    at_t = lax.broadcasted_iota(jnp.int32, (BLK, BLK), 0)
    at_s = lax.broadcasted_iota(jnp.int32, (BLK, BLK), 1)
    for b in range(nb):
        wide = jnp.concatenate([segcol[blk(b), :]] * (BLK // 128), axis=1)
        equal = wide == segrow[0:1, blk(b)]
        mask[b] = jnp.where(jnp.logical_and(equal, at_t >= at_s), 1.0, 0.0).astype(BF16)
        maskt[b] = jnp.where(jnp.logical_and(equal, at_s >= at_t), 1.0, 0.0).astype(BF16)

    whole_loads[0].wait()

    def inner(l, carry):
        for h in range(heads):
            for b in range(nb):
                scores = dot(q_ref[l, blk(b), hd(h)], k_ref[l, blk(b), hd(h)], 1, 1)
                weights = scores.astype(BF16) * mask[b]
                o_ref[l, blk(b), hd(h)] = dot(weights, v_ref[l, blk(b), hd(h)], 1, 0)
        return carry

    lax.fori_loop(0, layers, inner, 0)

    arrived(tabz.at[0 : nz - 1], tab_r)
    for l in range(layers):
        owner(0, l)

    before_chip = tabz[zmod(z - 1), 3:4, :]
    after_chip = tabz[zmod(z + 1), 0:1, :]
    before = jnp.where(is0, before_chip, last0)
    after = jnp.where(is0, first1, after_chip)
    prior = [before] + last[: nb - 1]
    later = first[1:] + [after]

    def prepare(l, carry):
        for b in range(nb):
            seen_f = column_mask(b, prior[b])
            seen_b = column_mask(b, later[b])
            head = column_mask(b, first[b])
            for h in range(heads):
                q = q_ref[l, blk(b), hd(h)]
                k = k_ref[l, blk(b), hd(h)]
                qs[l, blk(b), hd(h)] = q * seen_f
                qmt[l, hd(h), blk(b)] = (q * head).T
                ks[l, blk(b), hd(h)] = k * seen_b
                vs[l, blk(b), hd(h)] = v_ref[l, blk(b), hd(h)] * seen_b
                pt[l, h, b] = dot(k, q, 1, 1).astype(BF16) * maskt[b]
        return carry

    lax.fori_loop(0, layers, prepare, 0)

    whole_loads[1].wait()
    store_ks.start()
    store_vs.start()
    small[1].wait()
    joined = same(before_chip, last0)

    ones = jnp.ones((8, 2 * DH), BF16)

    def split(x):
        high = x.astype(BF16)
        return jnp.concatenate([high, (x - high.astype(F32)).astype(BF16)], axis=1)

    def carried(l):
        entered(0, l)
        for h in range(heads):
            state = dev[0, l, h]
            for b in range(nb):
                if b:
                    state = tails[l, h, b - 1] + same(prior[b - 1], prior[b]) * state
                cq[l, h, b] = state.astype(BF16)
        tiles = [jnp.zeros((8, 128), F32), jnp.zeros((8, 128), F32)]
        for b in range(nb):
            square, cross = None, None
            for h in range(heads):
                o = o_ref[l, blk(b), hd(h)] + dot(qs[l, blk(b), hd(h)], cq[l, h, b], 1, 0)
                o_ref[l, blk(b), hd(h)] = o
                a = g_ref[l, blk(b), hd(h)].astype(F32) * gain_ref[l : l + 1, hd(h)]
                square = o * o if square is None else square + o * o
                cross = a * o if cross is None else cross + a * o
            for n, x in enumerate((square, cross)):
                total = dot(ones, split(x), 1, 1)
                for i in range(BLK // 128):
                    tiles[n] = jnp.where(
                        tile_row == b * (BLK // 128) + i, total[:, 128 * i : 128 * (i + 1)], tiles[n]
                    )
        stat[l, f, 0:8, :] = tiles[0]
        stat[l, f, 8:16, :] = tiles[1]
        for j in range(1, nf):
            remote(stat.at[l, f], stat.at[l, f], st_s, st_r.at[l], fpeer(j)).start()

    for l in range(layers):
        entering(0, l, joined)
        if l > 0:
            carried(l - 1)
    carried(layers - 1)

    for l in range(layers):
        arrived(stat.at[l, 0 : nf - 1], st_r.at[l])
        both = stat[l, 0]
        for i in range(1, nf):
            both = both + stat[l, i]
        r = lax.rsqrt(both[0:8] / features + EPSILON)
        keep = keep_ref[l].astype(F32) / KEEP_RATE
        scale_a = keep * r
        scale_o = scale_a * (r * r) * (both[8:16] / features)
        turned = jnp.concatenate([scale_a, scale_o, jnp.zeros((112, 128), F32)], axis=0).T
        gains = [jnp.zeros((1, DH), F32) for h in range(heads)]
        totals = [None] * heads
        for b in range(nb):
            per = BLK // 128
            col_a = jnp.concatenate(
                [jnp.broadcast_to(turned[:, per * b + i : per * b + i + 1], (128, 128)) for i in range(per)], axis=0
            )
            col_o = jnp.concatenate(
                [jnp.broadcast_to(turned[:, 8 + per * b + i : 9 + per * b + i], (128, 128)) for i in range(per)], axis=0
            )
            for h in range(heads):
                o = o_ref[l, blk(b), hd(h)]
                up = g_ref[l, blk(b), hd(h)].astype(F32) * col_a
                gains[h] = gains[h] + jnp.sum(up * o, axis=0, keepdims=True)
                grad = (up * gain_ref[l : l + 1, hd(h)] - o * col_o).astype(BF16)
                do_ref[l, blk(b), hd(h)] = grad
                part = dot(qmt[l, hd(h), blk(b)], grad, 1, 0)
                fronts[l, h, b] = part
                part = part * same(first[b], first[0])
                totals[h] = part if totals[h] is None else totals[h] + part
        for h in range(heads):
            dsum[1, l, h] = totals[h]
            gtile[heads * l + h : heads * l + h + 1, :] = gains[h]
        hand_over(1, l)
        if l > 0:
            chip_total(1, l - 1, begin_own, begin_partner)
    for i in range(heads * layers, 8):
        gtile[i : i + 1, :] = jnp.zeros((1, DH), F32)
    remote(gtile, gptile, gt_s, gt_r, partner).start()
    chip_total(1, layers - 1, begin_own, begin_partner)

    def outer_head(l, h):
        for b in range(nb):
            grad = do_ref[l, blk(b), hd(h)]
            v = v_ref[l, blk(b), hd(h)]
            vpart[l, blk(b), hd(h)] = dot(pt[l, h, b], grad, 1, 0)
            gst = dot(v, grad, 1, 1).astype(BF16) * maskt[b]
            kpart[l, blk(b), hd(h)] = dot(gst, q_ref[l, blk(b), hd(h)], 1, 0)

    def outer(l, carry):
        for h in range(heads):
            outer_head(l, h)
        return carry

    lax.fori_loop(0, layers - 1, outer, 0)
    for h in range(heads - 1):
        outer_head(layers - 1, h)
    arrived(gptile, gt_r)
    gslots[z] = gtile[...] + gptile[...]
    for j in steps:
        remote(gslots.at[z], gslots.at[z], gz_s, gz_r, zpeer(j)).start()
    for l in range(layers - 1):
        owner(1, l)
    outer_head(layers - 1, heads - 1)
    owner(1, layers - 1)
    store_k.start()
    store_v.start()

    def outer_q(l, carry):
        for h in range(heads):
            for b in range(nb):
                grad = do_ref[l, blk(b), hd(h)]
                gs = dot(grad, v_ref[l, blk(b), hd(h)], 1, 1).astype(BF16) * mask[b]
                seen_f = column_mask(b, prior[b])
                dq_ref[l, blk(b), hd(h)] = (
                    dot(gs, k_ref[l, blk(b), hd(h)], 1, 0) + dot(grad * seen_f, cq[l, h, b], 1, 1)
                ).astype(BF16)
        return carry

    lax.fori_loop(0, layers, outer_q, 0)
    store_dq.start()
    sent(mytile, tile_s)
    sent(tabz.at[0 : nz - 1], tab_s)
    sent_state(0)
    sent(stat.at[:, 0 : nf - 1], st_s)
    sent(gtile, gt_s)

    joined = same(after_chip, first1)
    for l in range(layers):
        entering(1, l, joined)

    arrived(gslots.at[0 : nz - 1], gz_r)
    gtotal = gslots[0]
    for i in range(1, nz):
        gtotal = gtotal + gslots[i]
    for l in range(layers):
        for h in range(heads):
            gg_ref[l : l + 1, hd(h)] = gtotal[heads * l + h : heads * l + h + 1, :]
    small[2].start()
    sent(gslots.at[0 : nz - 1], gz_s)

    for l in range(layers):
        entered(1, l)
        for h in range(heads):
            state = dev[1, l, h]
            for b in range(nb)[::-1]:
                if b < nb - 1:
                    state = fronts[l, h, b + 1] + same(later[b + 1], later[b]) * state
                rq_ref[l, h, b] = state.astype(BF16)
    store_rq.start()
    sent_state(1)
    for copy in (store_ks, store_vs, store_k, store_v, store_dq, small[2], store_rq):
        copy.wait()


def finish(
    layers, rows, heads,
    dq_ref, kpart, vpart, ks, vs, rq, gg_ref,
    dq_hbm, dk_hbm, dv_hbm, gg_hbm,
    dk_ref, dv_ref, sem, gg_sem,
):
    nb = rows // BLK
    gg_copy = pltpu.make_async_copy(gg_ref, gg_hbm, gg_sem)
    gg_copy.start()

    def copy(i, ref, hbm, l):
        return pltpu.make_async_copy(ref.at[l], hbm.at[l], sem.at[i, l])

    for l in range(layers):
        copy(0, dq_ref, dq_hbm, l).start()
    for l in range(layers):
        for h in range(heads):
            for b in range(nb):
                at = (l, slice(BLK * b, BLK * (b + 1)), slice(DH * h, DH * (h + 1)))
                dk_ref[at] = (kpart[at] + dot(vs[at], rq[l, h, b], 1, 1)).astype(BF16)
                dv_ref[at] = (vpart[at] + dot(ks[at], rq[l, h, b], 1, 0)).astype(BF16)
        copy(1, dk_ref, dk_hbm, l).start()
        copy(2, dv_ref, dv_hbm, l).start()
    gg_copy.wait()
    for l in range(layers):
        copy(0, dq_ref, dq_hbm, l).wait()
        copy(1, dk_ref, dk_hbm, l).wait()
        copy(2, dv_ref, dv_hbm, l).wait()


def local(queries, keys, values, out_grad, gain, keep_mask, segments):
    layers, rows, channels = queries.shape
    heads = channels // DH
    nz = lax.axis_size("seq") // 2
    nf = lax.axis_size("fsdp")
    nb = rows // BLK
    cut = DH // nz
    whole = (layers, rows, channels)
    vmem = pltpu.VMEM
    dma = pltpu.SemaphoreType.DMA
    hbm = pl.BlockSpec(memory_space=pl.ANY)

    def far(x):
        return pltpu.with_memory_space_constraint(x, pltpu.HBM)

    near = pl.BlockSpec(memory_space=pltpu.VMEM)
    scratch = [
        vmem(whole, BF16), vmem(whole, BF16), vmem(whole, BF16), vmem(whole, BF16), dma((2, layers)), dma((2,)),
        vmem((layers, channels), F32), vmem((rows // 128, 128), jnp.int32), dma((3,)), dma((6,)),
        vmem(whole, BF16), vmem((layers, heads, nb, DH, DH), BF16), vmem((layers, channels), F32),
        vmem((1, rows), F32), vmem((rows, 128), F32), vmem((nb, BLK, BLK), BF16), vmem((nb, BLK, BLK), BF16),
        vmem((8, 128), F32), vmem((8, 128), F32), vmem((nz, 8, 128), F32),
        vmem((layers, heads, nb, DH, DH), F32), vmem((layers, heads, nb, DH, DH), F32),
        vmem((layers, heads, nb, DH, DH), BF16),
        vmem(whole, BF16), vmem((layers, channels, rows), BF16), vmem(whole, BF16), vmem(whole, BF16),
        vmem((layers, heads, nb, BLK, BLK), BF16),
        vmem(whole, F32), vmem(whole, BF16), vmem(whole, F32), vmem(whole, F32),
        vmem((2, layers, heads, DH, DH), F32), vmem((2, layers, DH, DH), F32), vmem((2, layers, DH, DH), F32),
        vmem((2, layers, nz, cut, DH), F32), vmem((2, layers, nz, cut, DH), F32),
        vmem((2, layers, DH, DH), F32), vmem((2, layers, DH, DH), F32), vmem((2, layers, heads, DH, DH), F32),
        vmem((layers, nf, 16, 128), F32),
        vmem((8, 128), F32), vmem((8, 128), F32), vmem((nz, 8, 128), F32),
        dma, dma, dma, dma,
        dma((2,)), dma((2, layers)),
        dma((2,)), dma((2, layers)),
        dma((2,)), dma((2, layers)),
        dma((2,)), dma((2, layers)),
        dma, dma((layers,)),
        dma, dma, dma, dma,
    ]
    results = pl.pallas_call(
        functools.partial(kernel, nz, nf, layers, rows, heads),
        out_shape=(
            vmem(whole, BF16),
            vmem(whole, F32),
            vmem(whole, F32),
            vmem(whole, BF16),
            vmem(whole, BF16),
            vmem((layers, heads, nb, DH, DH), BF16),
            vmem((layers, channels), F32),
        ),
        in_specs=[hbm, hbm, hbm, hbm, hbm, pl.BlockSpec(memory_space=pltpu.SMEM), hbm],
        out_specs=(hbm,) * 7,
        scratch_shapes=scratch,
        compiler_params=pltpu.CompilerParams(
            collective_id=0, has_side_effects=True, vmem_limit_bytes=44 * 2**20
        ),
        name="backward",
    )(
        far(queries), far(keys), far(values), far(out_grad), far(gain), keep_mask,
        far(segments.reshape(rows // 128, 128)),
    )
    return pl.pallas_call(
        functools.partial(finish, layers, rows, heads),
        out_shape=(
            jax.ShapeDtypeStruct(whole, BF16),
            jax.ShapeDtypeStruct(whole, BF16),
            jax.ShapeDtypeStruct(whole, BF16),
            jax.ShapeDtypeStruct((layers, channels), F32),
        ),
        in_specs=[near] * 7,
        out_specs=(hbm,) * 4,
        scratch_shapes=[vmem(whole, BF16), vmem(whole, BF16), dma((3, layers)), dma],
        compiler_params=pltpu.CompilerParams(vmem_limit_bytes=8 * 2**20),
        name="finish",
    )(*[pltpu.with_memory_space_constraint(result, pltpu.VMEM) for result in results])


def solution(mesh):
    wide = P(None, "seq", "fsdp")
    in_specs = (wide, wide, wide, wide, P(None, "fsdp"), P(), P("seq"))
    out_specs = (wide, wide, wide, P(None, "fsdp"))
    return jax.shard_map(local, mesh=mesh, in_specs=in_specs, out_specs=out_specs, check_vma=False)
```

time: 63.2 us -> 50.7 us (0.80)
  local copies, waits for them, and re-layouts: 6.49 us -> 0 us
  Pallas kernels: 55.9 us -> 50 us
    pallas_call x1, Pallas kernels: 55.9 us -> 47.7 us  [local(): pl.pallas_call(functools.partial(kernel, nz, nf, layers, rows, heads), ou...]
    unnamed x10 -> x0, local copies, waits for them, and re-layouts: 6.49 us -> none
    pallas_call x0 -> x1, Pallas kernels: none -> 2.27 us  [local(): pl.pallas_call(functools.partial(finish, layers, rows, heads), out_shape=...]
where the time goes in v2:
time: 50.7 us; the launch traced here: 50.6 us
  Pallas kernels  50 us (99%)
  between operations  0.64 us (1%)
    pallas_call x1, Pallas kernels, local(): pl.pallas_call(functools.partial(kernel, nz, nf, layers, rows, heads), ou...  47.7 us
    pallas_call x1, Pallas kernels, local(): pl.pallas_call(functools.partial(finish, layers, rows, heads), out_shape=...  2.27 us

profile of v2, /device:TPU:1, one launch (start us, length us, event | category | flops | bytes accessed | tf_op | source)
XLA Modules:
  0.0 50.6 jit_solution(6144013534892583755)
XLA Ops:
  0.6 47.7 %backward.1 = (bf16[3,1024,256]{2,1,0:T(8,128)(2,1)S(1)}, f32[3,1024,256]{2,1,0:T(8,128)S(1)}, f32[3,1024,256]{2,1,0:T(8,128)S(1)}, bf16[3,1024,256]{2,1,0:T(8,1...) custom-call(bf16[3,1024,256]{2,1,0:T(8,128)(2,1)} %q_hbm.1, ...), custom_call_target="tpu_custom_call" | custom-call | tf_op jit(solution)/shard_map/backward/pallas_call | solution.py:499
  48.3 2.3 %finish.1 = (bf16[3,1024,256]{2,1,0:T(8,128)(2,1)}, bf16[3,1024,256]{2,1,0:T(8,128)(2,1)}, bf16[3,1024,256]{2,1,0:T(8,128)(2,1)}, f32[3,256]{1,0:T(4,128)}) custom-call(bf16[3,1024,256]{2,1,0:T(8,128)(2,1)S(1)} %get-tuple-element.11.dq_ref, f32[3,1024,256]{2,1,0:T(8,128)S(1)} %get-tuple-element.12.kpart, f32[3,1024,256]{2,1,0:T(8,128)S(1)} %get-tuple-element.13.vpart, ...), custom_call_target="tpu_custom_call" | custom-call | tf_op jit(solution)/shard_map/finish/pallas_call | solution.py:521

commit v3 on v2

--- a/solution.py
+++ b/solution.py
@@ -1,4 +1,5 @@
 import functools
+import math
 
 import jax
 import jax.numpy as jnp
@@ -11,6 +12,7 @@
 BLK = 256
 EPSILON = 1e-06
 KEEP_RATE = 0.75
+LONGEST = 8192
 F32 = jnp.float32
 BF16 = jnp.bfloat16
 MESH = pl.DeviceIdType.MESH
@@ -26,20 +28,22 @@
 
 def kernel(
     nz, nf, layers, rows, heads,
-    q_hbm, k_hbm, v_hbm, g_hbm, gain_hbm, keep_ref, seg_hbm,
+    q_hbm, k_hbm, v_hbm, g_hbm, gain_hbm, keep_hbm, seg_hbm,
     dq_out, kpart_out, vpart_out, ks_out, vs_out, rq_out, gg_out,
-    q_ref, k_ref, v_ref, g_ref, ld_sem, qg_sem, gain_ref, seg_ref, small_sem, out_sem,
+    q_ref, k_ref, v_ref, g_ref, ld_sem, qg_sem, gain_ref, seg_ref, keep_ref, small_sem, out_sem,
     dq_ref, rq_ref, gg_ref,
     segrow, segcol, mask, maskt, mytile, ptile, tabz,
     tails, fronts, cq, qs, qmt, ks, vs, pt, o_ref, do_ref, kpart, vpart,
     dsum, dpart, tot, slots, ebuf, ein, xbuf, dev,
-    stat, gtile, gptile, gslots,
+    stat, gain8, gain_sum, gtile, gptile, gslots,
     tile_s, tile_r, tab_s, tab_r,
-    d_s, d_r, a_s, a_r, e_s, e_r, x_s, x_r,
+    d_s, d_r, a_s, a_r, b_r, e_s, e_r, x_s, x_r,
     st_s, st_r, gt_s, gt_r, gz_s, gz_r,
 ):
     nb = rows // BLK
     cut = DH // nz
+    opposite = nz // 2
+    reach = min(nz - 1, -(-LONGEST // (2 * rows)))
     steps = sorted(range(1, nz), key=lambda j: -min(j, nz - j))
     features = heads * DH * nf
     s = lax.axis_index("seq")
@@ -54,8 +58,12 @@
     def zpeer(j):
         return (2 * zmod(z + j) + c, f)
 
-    def fpeer(j):
-        return (s, lax.rem(f + j, nf))
+    side = math.isqrt(nf)
+    others = [(j // side, j % side) for j in range(1, nf)]
+    others.sort(key=lambda d: -min(d[0], side - d[0]) - min(d[1], side - d[1]))
+
+    def fpeer(d):
+        return (s, lax.rem(f // side + d[0], side) * side + lax.rem(f % side + d[1], side))
 
     def remote(src, dst, ss, rs, to):
         return pltpu.make_async_remote_copy(
@@ -75,6 +83,7 @@
         pltpu.make_async_copy(seg_hbm, seg_ref, small_sem.at[0]),
         pltpu.make_async_copy(gain_hbm, gain_ref, small_sem.at[1]),
         pltpu.make_async_copy(gg_ref, gg_out, small_sem.at[2]),
+        pltpu.make_async_copy(keep_hbm, keep_ref, small_sem.at[3]),
     )
     small[0].start()
     load(0, k_hbm, k_ref, 0).start()
@@ -93,11 +102,11 @@
     )
 
     barrier = pltpu.get_barrier_semaphore()
+    for j in steps:
+        pl.semaphore_signal(barrier, inc=1, device_id=zpeer(j), device_id_type=MESH)
+    for j in others:
+        pl.semaphore_signal(barrier, inc=1, device_id=fpeer(j), device_id_type=MESH)
     pl.semaphore_signal(barrier, inc=1, device_id=partner, device_id_type=MESH)
-    for j in range(1, nz):
-        pl.semaphore_signal(barrier, inc=1, device_id=zpeer(j), device_id_type=MESH)
-    for j in range(1, nf):
-        pl.semaphore_signal(barrier, inc=1, device_id=fpeer(j), device_id_type=MESH)
 
     small[0].wait()
     for l in range(1, layers):
@@ -123,6 +132,9 @@
     def column_mask(b, value):
         return same(segcol[blk(b), :], value).astype(BF16)
 
+    def wide_mask(b, value):
+        return jnp.concatenate([column_mask(b, value)] * heads, axis=1)
+
     def hand_over(w, l):
         remote(dsum.at[w, l, 1 - c], dpart.at[w, l], d_s.at[w], d_r.at[w, l], partner).start()
 
@@ -132,33 +144,51 @@
         tot[w, l] = total
         for j in steps:
             at = pl.multiple_of(zmod(z + j) * cut, cut)
+            into = b_r if j == opposite else a_r
             remote(
-                tot.at[w, l, pl.ds(at, cut)], slots.at[w, l, z], a_s.at[w], a_r.at[w, l], zpeer(j)
+                tot.at[w, l, pl.ds(at, cut)], slots.at[w, l, z], a_s.at[w], into.at[w, l], zpeer(j)
             ).start()
         slots[w, l, z] = tot[w, l, pl.ds(pl.multiple_of(z * cut, cut), cut)]
 
-    def owner(w, l):
-        arrived(slots.at[w, l, 0 : nz - 1], a_r.at[w, l])
-        if w == 0:
-            edge = [tabz[i, 3:4, :] for i in range(nz)]
-            order = list(range(nz))
-        else:
-            edge = [tabz[i, 0:1, :] for i in range(nz)]
-            order = list(range(nz))[::-1]
-        state = jnp.zeros((cut, DH), F32)
-        for n, i in enumerate(order):
-            if n == 1:
-                state = slots[w, l, order[0]]
-            elif n > 1:
-                state = slots[w, l, order[n - 1]] + same(edge[order[n - 2]], edge[order[n - 1]]) * state
-            ebuf[w, l, i] = state
-        for j in steps:
-            remote(
-                ebuf.at[w, l, zmod(z + j)],
-                ein.at[w, l, pl.ds(pl.multiple_of(z * cut, cut), cut)],
-                e_s.at[w], e_r.at[w, l], zpeer(j),
-            ).start()
-        ein[w, l, pl.ds(pl.multiple_of(z * cut, cut), cut)] = ebuf[w, l, z]
+    def owner_weights(w):
+        row = 3 if w == 0 else 0
+        side = -1 if w == 0 else 1
+        weights = {}
+        for r in range(nz):
+            target = zmod(z + r)
+            nearest = tabz[zmod(target + side), row : row + 1, :]
+            for i in range(1, reach + 1):
+                source = target + side * i
+                inside = jnp.logical_and(source >= 0, source < nz)
+                weight = same(tabz[zmod(source), row : row + 1, :], nearest)
+                weights[r, i] = jnp.where(inside, weight, 0.0)
+        return weights
+
+    def owner(w, l, weights):
+        side = -1 if w == 0 else 1
+
+        def state(r):
+            total = None
+            for i in range(1, reach + 1):
+                term = weights[r, i] * slots[w, l, zmod(z + r + side * i)]
+                total = term if total is None else total + term
+            return total
+
+        def far_use(r):
+            return any((r + side * i - opposite) % nz == 0 for i in range(1, reach + 1))
+
+        here = pl.ds(pl.multiple_of(z * cut, cut), cut)
+        arrived(slots.at[w, l, 0 : nz - 2], a_r.at[w, l])
+        for late in (False, True):
+            if late:
+                arrived(slots.at[w, l, 0], b_r.at[w, l])
+            for r in steps:
+                if far_use(r) == late:
+                    ebuf[w, l, zmod(z + r)] = state(r)
+                    remote(
+                        ebuf.at[w, l, zmod(z + r)], ein.at[w, l, here], e_s.at[w], e_r.at[w, l], zpeer(r)
+                    ).start()
+        ein[w, l, here] = state(0)
 
     def entering(w, l, joined):
         arrived(ein.at[w, l, 0 : DH - cut], e_r.at[w, l])
@@ -182,18 +212,23 @@
         sent(ebuf.at[w, :, 0 : nz - 1], e_s.at[w])
         sent(xbuf.at[w], x_s.at[w])
 
-    tail_masks = [column_mask(b, last[b]) for b in range(nb)]
-    for l in range(layers):
+    tail_masks = [wide_mask(b, last[b]) for b in range(nb)]
+    def tails_of(l, carry):
         load(0, k_hbm, k_ref, l).wait()
         load(1, v_hbm, v_ref, l).wait()
-        for h in range(heads):
-            total = None
-            for b in range(nb):
-                part = dot(k_ref[l, blk(b), hd(h)], v_ref[l, blk(b), hd(h)] * tail_masks[b], 0, 0)
+        totals = [None] * heads
+        for b in range(nb):
+            both = dot(k_ref[l, blk(b), :], v_ref[l, blk(b), :] * tail_masks[b], 0, 0)
+            for h in range(heads):
+                part = both[hd(h), hd(h)]
                 tails[l, h, b] = part
                 part = part * same(last[b], last[nb - 1])
-                total = part if total is None else total + part
-            dsum[0, l, h] = total
+                totals[h] = part if totals[h] is None else totals[h] + part
+        for h in range(heads):
+            dsum[0, l, h] = totals[h]
+        return carry
+
+    lax.fori_loop(0, layers, tails_of, 0)
     pl.semaphore_wait(barrier, 1 + (nz - 1) + (nf - 1))
     remote(mytile, ptile, tile_s, tile_r, partner).start()
     for l in range(layers):
@@ -201,6 +236,7 @@
     for copy in whole_loads:
         copy.start()
     small[1].start()
+    small[3].start()
 
     arrived(ptile, tile_r)
     chiptile = mytile[...] + ptile[...]
@@ -225,6 +261,11 @@
         mask[b] = jnp.where(jnp.logical_and(equal, at_t >= at_s), 1.0, 0.0).astype(BF16)
         maskt[b] = jnp.where(jnp.logical_and(equal, at_s >= at_t), 1.0, 0.0).astype(BF16)
 
+    for l in range(layers):
+        for b in range(nb):
+            cq[l, b] = jnp.zeros((heads * DH, heads * DH), BF16)
+            rq_ref[l, b] = jnp.zeros((heads * DH, heads * DH), BF16)
+
     whole_loads[0].wait()
 
     def inner(l, carry):
@@ -238,8 +279,9 @@
     lax.fori_loop(0, layers, inner, 0)
 
     arrived(tabz.at[0 : nz - 1], tab_r)
-    for l in range(layers):
-        owner(0, l)
+    weights = owner_weights(0)
+    for l in range(layers):
+        owner(0, l, weights)
 
     before_chip = tabz[zmod(z - 1), 3:4, :]
     after_chip = tabz[zmod(z + 1), 0:1, :]
@@ -269,13 +311,12 @@
     store_ks.start()
     store_vs.start()
     small[1].wait()
+    small[3].wait()
+    for l in range(layers):
+        gain8[l] = jnp.broadcast_to(gain_ref[l : l + 1, :], (8, heads * DH))
     joined = same(before_chip, last0)
 
-    ones = jnp.ones((8, 2 * DH), BF16)
-
-    def split(x):
-        high = x.astype(BF16)
-        return jnp.concatenate([high, (x - high.astype(F32)).astype(BF16)], axis=1)
+    diagonal = lax.broadcasted_iota(jnp.int32, (128, 128), 0) == lax.broadcasted_iota(jnp.int32, (128, 128), 1)
 
     def carried(l):
         entered(0, l)
@@ -284,25 +325,24 @@
             for b in range(nb):
                 if b:
                     state = tails[l, h, b - 1] + same(prior[b - 1], prior[b]) * state
-                cq[l, h, b] = state.astype(BF16)
-        tiles = [jnp.zeros((8, 128), F32), jnp.zeros((8, 128), F32)]
+                cq[l, b, hd(h), hd(h)] = state.astype(BF16)
+        tiles = [[], []]
         for b in range(nb):
             square, cross = None, None
+            out = o_ref[l, blk(b), :] + dot(qs[l, blk(b), :], cq[l, b], 1, 0)
+            o_ref[l, blk(b), :] = out
             for h in range(heads):
-                o = o_ref[l, blk(b), hd(h)] + dot(qs[l, blk(b), hd(h)], cq[l, h, b], 1, 0)
-                o_ref[l, blk(b), hd(h)] = o
-                a = g_ref[l, blk(b), hd(h)].astype(F32) * gain_ref[l : l + 1, hd(h)]
+                o = out[:, hd(h)]
+                a = g_ref[l, blk(b), hd(h)].astype(F32) * gain8[l, 0:1, hd(h)]
                 square = o * o if square is None else square + o * o
                 cross = a * o if cross is None else cross + a * o
             for n, x in enumerate((square, cross)):
-                total = dot(ones, split(x), 1, 1)
+                total = jnp.sum(x, axis=1, keepdims=True)
                 for i in range(BLK // 128):
-                    tiles[n] = jnp.where(
-                        tile_row == b * (BLK // 128) + i, total[:, 128 * i : 128 * (i + 1)], tiles[n]
-                    )
-        stat[l, f, 0:8, :] = tiles[0]
-        stat[l, f, 8:16, :] = tiles[1]
-        for j in range(1, nf):
+                    picked = jnp.where(diagonal, total[128 * i : 128 * (i + 1)], 0.0)
+                    tiles[n].append(jnp.sum(picked, axis=0, keepdims=True))
+        stat[l, f] = jnp.concatenate(tiles[0] + tiles[1], axis=0)
+        for j in others:
             remote(stat.at[l, f], stat.at[l, f], st_s, st_r.at[l], fpeer(j)).start()
 
     for l in range(layers):
@@ -311,15 +351,15 @@
             carried(l - 1)
     carried(layers - 1)
 
-    for l in range(layers):
+    def gradient(l, carry):
         arrived(stat.at[l, 0 : nf - 1], st_r.at[l])
-        both = stat[l, 0]
+        summed = stat[l, 0]
         for i in range(1, nf):
-            both = both + stat[l, i]
-        r = lax.rsqrt(both[0:8] / features + EPSILON)
+            summed = summed + stat[l, i]
+        r = lax.rsqrt(summed[0:8] / features + EPSILON)
         keep = keep_ref[l].astype(F32) / KEEP_RATE
         scale_a = keep * r
-        scale_o = scale_a * (r * r) * (both[8:16] / features)
+        scale_o = scale_a * (r * r) * (summed[8:16] / features)
         turned = jnp.concatenate([scale_a, scale_o, jnp.zeros((112, 128), F32)], axis=0).T
         gains = [jnp.zeros((1, DH), F32) for h in range(heads)]
         totals = [None] * heads
@@ -335,18 +375,29 @@
                 o = o_ref[l, blk(b), hd(h)]
                 up = g_ref[l, blk(b), hd(h)].astype(F32) * col_a
                 gains[h] = gains[h] + jnp.sum(up * o, axis=0, keepdims=True)
-                grad = (up * gain_ref[l : l + 1, hd(h)] - o * col_o).astype(BF16)
+                grad = (up * gain8[l, 0:1, hd(h)] - o * col_o).astype(BF16)
                 do_ref[l, blk(b), hd(h)] = grad
-                part = dot(qmt[l, hd(h), blk(b)], grad, 1, 0)
+            both = dot(qmt[l, :, blk(b)], do_ref[l, blk(b), :], 1, 0)
+            for h in range(heads):
+                part = both[hd(h), hd(h)]
                 fronts[l, h, b] = part
                 part = part * same(first[b], first[0])
                 totals[h] = part if totals[h] is None else totals[h] + part
         for h in range(heads):
             dsum[1, l, h] = totals[h]
-            gtile[heads * l + h : heads * l + h + 1, :] = gains[h]
+            gain_sum[l, h] = jnp.broadcast_to(gains[h], (8, DH))
         hand_over(1, l)
-        if l > 0:
+
+        @pl.when(l > 0)
+        def _():
             chip_total(1, l - 1, begin_own, begin_partner)
+
+        return carry
+
+    lax.fori_loop(0, layers, gradient, 0)
+    for l in range(layers):
+        for h in range(heads):
+            gtile[heads * l + h : heads * l + h + 1, :] = gain_sum[l, h, 0:1, :]
     for i in range(heads * layers, 8):
         gtile[i : i + 1, :] = jnp.zeros((1, DH), F32)
     remote(gtile, gptile, gt_s, gt_r, partner).start()
@@ -365,28 +416,32 @@
             outer_head(l, h)
         return carry
 
-    lax.fori_loop(0, layers - 1, outer, 0)
-    for h in range(heads - 1):
-        outer_head(layers - 1, h)
+    lax.fori_loop(0, layers - 2, outer, 0)
+    outer_head(layers - 2, 0)
     arrived(gptile, gt_r)
     gslots[z] = gtile[...] + gptile[...]
     for j in steps:
         remote(gslots.at[z], gslots.at[z], gz_s, gz_r, zpeer(j)).start()
-    for l in range(layers - 1):
-        owner(1, l)
-    outer_head(layers - 1, heads - 1)
-    owner(1, layers - 1)
+    weights = owner_weights(1)
+    for l in range(layers - 2):
+        owner(1, l, weights)
+    for h in range(1, heads):
+        outer_head(layers - 2, h)
+    owner(1, layers - 2, weights)
+    outer_head(layers - 1, 0)
+    owner(1, layers - 1, weights)
+    for h in range(1, heads):
+        outer_head(layers - 1, h)
     store_k.start()
     store_v.start()
 
     def outer_q(l, carry):
-        for h in range(heads):
-            for b in range(nb):
-                grad = do_ref[l, blk(b), hd(h)]
-                gs = dot(grad, v_ref[l, blk(b), hd(h)], 1, 1).astype(BF16) * mask[b]
-                seen_f = column_mask(b, prior[b])
+        for b in range(nb):
+            carry_part = dot(do_ref[l, blk(b), :] * wide_mask(b, prior[b]), cq[l, b], 1, 1)
+            for h in range(heads):
+                gs = dot(do_ref[l, blk(b), hd(h)], v_ref[l, blk(b), hd(h)], 1, 1).astype(BF16) * mask[b]
                 dq_ref[l, blk(b), hd(h)] = (
-                    dot(gs, k_ref[l, blk(b), hd(h)], 1, 0) + dot(grad * seen_f, cq[l, h, b], 1, 1)
+                    dot(gs, k_ref[l, blk(b), hd(h)], 1, 0) + carry_part[:, hd(h)]
                 ).astype(BF16)
         return carry
 
@@ -419,7 +474,7 @@
             for b in range(nb)[::-1]:
                 if b < nb - 1:
                     state = fronts[l, h, b + 1] + same(later[b + 1], later[b]) * state
-                rq_ref[l, h, b] = state.astype(BF16)
+                rq_ref[l, b, hd(h), hd(h)] = state.astype(BF16)
     store_rq.start()
     sent_state(1)
     for copy in (store_ks, store_vs, store_k, store_v, store_dq, small[2], store_rq):
@@ -442,11 +497,10 @@
     for l in range(layers):
         copy(0, dq_ref, dq_hbm, l).start()
     for l in range(layers):
-        for h in range(heads):
-            for b in range(nb):
-                at = (l, slice(BLK * b, BLK * (b + 1)), slice(DH * h, DH * (h + 1)))
-                dk_ref[at] = (kpart[at] + dot(vs[at], rq[l, h, b], 1, 1)).astype(BF16)
-                dv_ref[at] = (vpart[at] + dot(ks[at], rq[l, h, b], 1, 0)).astype(BF16)
+        for b in range(nb):
+            at = (l, slice(BLK * b, BLK * (b + 1)))
+            dk_ref[at] = (kpart[at] + dot(vs[at], rq[l, b], 1, 1)).astype(BF16)
+            dv_ref[at] = (vpart[at] + dot(ks[at], rq[l, b], 1, 0)).astype(BF16)
         copy(1, dk_ref, dk_hbm, l).start()
         copy(2, dv_ref, dv_hbm, l).start()
     gg_copy.wait()
@@ -474,23 +528,24 @@
     near = pl.BlockSpec(memory_space=pltpu.VMEM)
     scratch = [
         vmem(whole, BF16), vmem(whole, BF16), vmem(whole, BF16), vmem(whole, BF16), dma((2, layers)), dma((2,)),
-        vmem((layers, channels), F32), vmem((rows // 128, 128), jnp.int32), dma((3,)), dma((6,)),
-        vmem(whole, BF16), vmem((layers, heads, nb, DH, DH), BF16), vmem((layers, channels), F32),
+        vmem((layers, channels), F32), vmem((rows // 128, 128), jnp.int32),
+        pltpu.SMEM((layers,), jnp.int32), dma((4,)), dma((6,)),
+        vmem(whole, BF16), vmem((layers, nb, channels, channels), BF16), vmem((layers, channels), F32),
         vmem((1, rows), F32), vmem((rows, 128), F32), vmem((nb, BLK, BLK), BF16), vmem((nb, BLK, BLK), BF16),
         vmem((8, 128), F32), vmem((8, 128), F32), vmem((nz, 8, 128), F32),
         vmem((layers, heads, nb, DH, DH), F32), vmem((layers, heads, nb, DH, DH), F32),
-        vmem((layers, heads, nb, DH, DH), BF16),
+        vmem((layers, nb, channels, channels), BF16),
         vmem(whole, BF16), vmem((layers, channels, rows), BF16), vmem(whole, BF16), vmem(whole, BF16),
         vmem((layers, heads, nb, BLK, BLK), BF16),
         vmem(whole, F32), vmem(whole, BF16), vmem(whole, F32), vmem(whole, F32),
         vmem((2, layers, heads, DH, DH), F32), vmem((2, layers, DH, DH), F32), vmem((2, layers, DH, DH), F32),
         vmem((2, layers, nz, cut, DH), F32), vmem((2, layers, nz, cut, DH), F32),
         vmem((2, layers, DH, DH), F32), vmem((2, layers, DH, DH), F32), vmem((2, layers, heads, DH, DH), F32),
-        vmem((layers, nf, 16, 128), F32),
+        vmem((layers, nf, 16, 128), F32), vmem((layers, 8, channels), F32), vmem((layers, heads, 8, DH), F32),
         vmem((8, 128), F32), vmem((8, 128), F32), vmem((nz, 8, 128), F32),
         dma, dma, dma, dma,
         dma((2,)), dma((2, layers)),
-        dma((2,)), dma((2, layers)),
+        dma((2,)), dma((2, layers)), dma((2, layers)),
         dma((2,)), dma((2, layers)),
         dma((2,)), dma((2, layers)),
         dma, dma((layers,)),
@@ -504,10 +559,10 @@
             vmem(whole, F32),
             vmem(whole, BF16),
             vmem(whole, BF16),
-            vmem((layers, heads, nb, DH, DH), BF16),
+            vmem((layers, nb, channels, channels), BF16),
             vmem((layers, channels), F32),
         ),
-        in_specs=[hbm, hbm, hbm, hbm, hbm, pl.BlockSpec(memory_space=pltpu.SMEM), hbm],
+        in_specs=[hbm] * 7,
         out_specs=(hbm,) * 7,
         scratch_shapes=scratch,
         compiler_params=pltpu.CompilerParams(
@@ -515,7 +570,7 @@
         ),
         name="backward",
     )(
-        far(queries), far(keys), far(values), far(out_grad), far(gain), keep_mask,
+        far(queries), far(keys), far(values), far(out_grad), far(gain), far(keep_mask),
         far(segments.reshape(rows // 128, 128)),
     )
     return pl.pallas_call(

time: 50.7 us -> 48.4 us (0.955)
  Pallas kernels: 50 us -> 47.6 us
    pallas_call x1, Pallas kernels: 47.7 us -> 45.3 us  [local(): pl.pallas_call(functools.partial(kernel, nz, nf, layers, rows, heads), ou...]
where the time goes in v3:
time: 48.4 us; the launch traced here: 48.3 us
  Pallas kernels  47.6 us (98%)
  between operations  0.64 us (1%)
    pallas_call x1, Pallas kernels, local(): pl.pallas_call(functools.partial(kernel, nz, nf, layers, rows, heads), ou...  45.3 us
    pallas_call x1, Pallas kernels, local(): pl.pallas_call(functools.partial(finish, layers, rows, heads), out_shape=...  2.28 us

profile of v3, /device:TPU:1, one launch (start us, length us, event | category | flops | bytes accessed | tf_op | source)
XLA Modules:
  0.0 48.3 jit_solution(17449699499369737814)
XLA Ops:
  0.6 45.3 %backward.1 = (bf16[3,1024,256]{2,1,0:T(8,128)(2,1)S(1)}, f32[3,1024,256]{2,1,0:T(8,128)S(1)}, f32[3,1024,256]{2,1,0:T(8,128)S(1)}, bf16[3,1024,256]{2,1,0:T(8,1...) custom-call(bf16[3,1024,256]{2,1,0:T(8,128)(2,1)} %q_hbm.1, ...), custom_call_target="tpu_custom_call" | custom-call | tf_op jit(solution)/shard_map/backward/pallas_call | solution.py:554
  46.0 2.3 %finish.1 = (bf16[3,1024,256]{2,1,0:T(8,128)(2,1)}, bf16[3,1024,256]{2,1,0:T(8,128)(2,1)}, bf16[3,1024,256]{2,1,0:T(8,128)(2,1)}, f32[3,256]{1,0:T(4,128)}) custom-call(bf16[3,1024,256]{2,1,0:T(8,128)(2,1)S(1)} %get-tuple-element.11.dq_ref, f32[3,1024,256]{2,1,0:T(8,128)S(1)} %get-tuple-element.12.kpart, f32[3,1024,256]{2,1,0:T(8,128)S(1)} %get-tuple-element.13.vpart, ...), custom_call_target="tpu_custom_call" | custom-call | tf_op jit(solution)/shard_map/finish/pallas_call | solution.py:576

commit v4 on v3

--- a/solution.py
+++ b/solution.py
@@ -151,7 +151,7 @@
         slots[w, l, z] = tot[w, l, pl.ds(pl.multiple_of(z * cut, cut), cut)]
 
     def owner_weights(w):
-        row = 3 if w == 0 else 0
+        row = 1 if w == 0 else 0
         side = -1 if w == 0 else 1
         weights = {}
         for r in range(nz):
@@ -240,7 +240,7 @@
 
     arrived(ptile, tile_r)
     chiptile = mytile[...] + ptile[...]
-    tabz[z] = chiptile
+    tabz[z] = jnp.concatenate([chiptile[0:1], chiptile[3:4]], axis=0)
     for j in steps:
         remote(tabz.at[z], tabz.at[z], tab_s, tab_r, zpeer(j)).start()
     first0, last0 = chiptile[0:1], chiptile[1:2]
@@ -264,7 +264,6 @@
     for l in range(layers):
         for b in range(nb):
             cq[l, b] = jnp.zeros((heads * DH, heads * DH), BF16)
-            rq_ref[l, b] = jnp.zeros((heads * DH, heads * DH), BF16)
 
     whole_loads[0].wait()
 
@@ -278,35 +277,38 @@
 
     lax.fori_loop(0, layers, inner, 0)
 
+    def prepare(l, carry):
+        for b in range(nb):
+            qmt[l, :, blk(b)] = (q_ref[l, blk(b), :] * wide_mask(b, first[b])).T
+            for h in range(heads):
+                pt[l, h, b] = (
+                    dot(k_ref[l, blk(b), hd(h)], q_ref[l, blk(b), hd(h)], 1, 1).astype(BF16) * maskt[b]
+                )
+        return carry
+
+    lax.fori_loop(0, layers, prepare, 0)
+
     arrived(tabz.at[0 : nz - 1], tab_r)
     weights = owner_weights(0)
     for l in range(layers):
         owner(0, l, weights)
 
-    before_chip = tabz[zmod(z - 1), 3:4, :]
+    before_chip = tabz[zmod(z - 1), 1:2, :]
     after_chip = tabz[zmod(z + 1), 0:1, :]
     before = jnp.where(is0, before_chip, last0)
     after = jnp.where(is0, first1, after_chip)
     prior = [before] + last[: nb - 1]
     later = first[1:] + [after]
 
-    def prepare(l, carry):
-        for b in range(nb):
-            seen_f = column_mask(b, prior[b])
-            seen_b = column_mask(b, later[b])
-            head = column_mask(b, first[b])
-            for h in range(heads):
-                q = q_ref[l, blk(b), hd(h)]
-                k = k_ref[l, blk(b), hd(h)]
-                qs[l, blk(b), hd(h)] = q * seen_f
-                qmt[l, hd(h), blk(b)] = (q * head).T
-                ks[l, blk(b), hd(h)] = k * seen_b
-                vs[l, blk(b), hd(h)] = v_ref[l, blk(b), hd(h)] * seen_b
-                pt[l, h, b] = dot(k, q, 1, 1).astype(BF16) * maskt[b]
+    def select(l, carry):
+        for b in range(nb):
+            qs[l, blk(b), :] = q_ref[l, blk(b), :] * wide_mask(b, prior[b])
+            seen_b = wide_mask(b, later[b])
+            ks[l, blk(b), :] = k_ref[l, blk(b), :] * seen_b
+            vs[l, blk(b), :] = v_ref[l, blk(b), :] * seen_b
         return carry
 
-    lax.fori_loop(0, layers, prepare, 0)
-
+    lax.fori_loop(0, layers, select, 0)
     whole_loads[1].wait()
     store_ks.start()
     store_vs.start()
@@ -416,25 +418,6 @@
             outer_head(l, h)
         return carry
 
-    lax.fori_loop(0, layers - 2, outer, 0)
-    outer_head(layers - 2, 0)
-    arrived(gptile, gt_r)
-    gslots[z] = gtile[...] + gptile[...]
-    for j in steps:
-        remote(gslots.at[z], gslots.at[z], gz_s, gz_r, zpeer(j)).start()
-    weights = owner_weights(1)
-    for l in range(layers - 2):
-        owner(1, l, weights)
-    for h in range(1, heads):
-        outer_head(layers - 2, h)
-    owner(1, layers - 2, weights)
-    outer_head(layers - 1, 0)
-    owner(1, layers - 1, weights)
-    for h in range(1, heads):
-        outer_head(layers - 1, h)
-    store_k.start()
-    store_v.start()
-
     def outer_q(l, carry):
         for b in range(nb):
             carry_part = dot(do_ref[l, blk(b), :] * wide_mask(b, prior[b]), cq[l, b], 1, 1)
@@ -445,7 +428,38 @@
                 ).astype(BF16)
         return carry
 
-    lax.fori_loop(0, layers, outer_q, 0)
+    lax.fori_loop(0, layers - 2, outer, 0)
+    outer_q(0, 0)
+    arrived(gptile, gt_r)
+    gslots[z] = gtile[...] + gptile[...]
+    weights = owner_weights(1)
+    for l in range(layers - 2):
+        owner(1, l, weights)
+    outer_head(layers - 2, 0)
+    owner(1, layers - 2, weights)
+    for h in range(1, heads):
+        outer_head(layers - 2, h)
+    owner(1, layers - 1, weights)
+    for j in steps:
+        remote(gslots.at[z], gslots.at[z], gz_s, gz_r, zpeer(j)).start()
+    lax.fori_loop(layers - 1, layers, outer, 0)
+    store_k.start()
+    store_v.start()
+
+    def later_states(l):
+        entered(1, l)
+        for h in range(heads):
+            state = dev[1, l, h]
+            for b in range(nb)[::-1]:
+                if b < nb - 1:
+                    state = fronts[l, h, b + 1] + same(later[b + 1], later[b]) * state
+                rq_ref[l, h, b] = state.astype(BF16)
+        pltpu.make_async_copy(rq_ref.at[l], rq_out.at[l], out_sem.at[5]).start()
+
+    joined = same(after_chip, first1)
+    for l in range(1, layers):
+        outer_q(l, 0)
+        entering(1, l - 1, joined)
     store_dq.start()
     sent(mytile, tile_s)
     sent(tabz.at[0 : nz - 1], tab_s)
@@ -453,10 +467,11 @@
     sent(stat.at[:, 0 : nf - 1], st_s)
     sent(gtile, gt_s)
 
-    joined = same(after_chip, first1)
-    for l in range(layers):
-        entering(1, l, joined)
-
+    for l in range(layers - 2):
+        later_states(l)
+    entering(1, layers - 1, joined)
+    for l in range(max(0, layers - 2), layers):
+        later_states(l)
     arrived(gslots.at[0 : nz - 1], gz_r)
     gtotal = gslots[0]
     for i in range(1, nz):
@@ -466,16 +481,6 @@
             gg_ref[l : l + 1, hd(h)] = gtotal[heads * l + h : heads * l + h + 1, :]
     small[2].start()
     sent(gslots.at[0 : nz - 1], gz_s)
-
-    for l in range(layers):
-        entered(1, l)
-        for h in range(heads):
-            state = dev[1, l, h]
-            for b in range(nb)[::-1]:
-                if b < nb - 1:
-                    state = fronts[l, h, b + 1] + same(later[b + 1], later[b]) * state
-                rq_ref[l, b, hd(h), hd(h)] = state.astype(BF16)
-    store_rq.start()
     sent_state(1)
     for copy in (store_ks, store_vs, store_k, store_v, store_dq, small[2], store_rq):
         copy.wait()
@@ -498,9 +503,10 @@
         copy(0, dq_ref, dq_hbm, l).start()
     for l in range(layers):
         for b in range(nb):
-            at = (l, slice(BLK * b, BLK * (b + 1)))
-            dk_ref[at] = (kpart[at] + dot(vs[at], rq[l, b], 1, 1)).astype(BF16)
-            dv_ref[at] = (vpart[at] + dot(ks[at], rq[l, b], 1, 0)).astype(BF16)
+            for h in range(heads):
+                at = (l, slice(BLK * b, BLK * (b + 1)), slice(DH * h, DH * (h + 1)))
+                dk_ref[at] = (kpart[at] + dot(vs[at], rq[l, h, b], 1, 1)).astype(BF16)
+                dv_ref[at] = (vpart[at] + dot(ks[at], rq[l, h, b], 1, 0)).astype(BF16)
         copy(1, dk_ref, dk_hbm, l).start()
         copy(2, dv_ref, dv_hbm, l).start()
     gg_copy.wait()
@@ -530,9 +536,9 @@
         vmem(whole, BF16), vmem(whole, BF16), vmem(whole, BF16), vmem(whole, BF16), dma((2, layers)), dma((2,)),
         vmem((layers, channels), F32), vmem((rows // 128, 128), jnp.int32),
         pltpu.SMEM((layers,), jnp.int32), dma((4,)), dma((6,)),
-        vmem(whole, BF16), vmem((layers, nb, channels, channels), BF16), vmem((layers, channels), F32),
+        vmem(whole, BF16), vmem((layers, heads, nb, DH, DH), BF16), vmem((layers, channels), F32),
         vmem((1, rows), F32), vmem((rows, 128), F32), vmem((nb, BLK, BLK), BF16), vmem((nb, BLK, BLK), BF16),
-        vmem((8, 128), F32), vmem((8, 128), F32), vmem((nz, 8, 128), F32),
+        vmem((8, 128), F32), vmem((8, 128), F32), vmem((nz, 2, 128), F32),
         vmem((layers, heads, nb, DH, DH), F32), vmem((layers, heads, nb, DH, DH), F32),
         vmem((layers, nb, channels, channels), BF16),
         vmem(whole, BF16), vmem((layers, channels, rows), BF16), vmem(whole, BF16), vmem(whole, BF16),
@@ -559,7 +565,7 @@
             vmem(whole, F32),
             vmem(whole, BF16),
             vmem(whole, BF16),
-            vmem((layers, nb, channels, channels), BF16),
+            vmem((layers, heads, nb, DH, DH), BF16),
             vmem((layers, channels), F32),
         ),
         in_specs=[hbm] * 7,

time: 48.4 us -> 47.9 us (0.990)
  Pallas kernels: 47.6 us -> 47 us
    pallas_call x1, Pallas kernels: 45.3 us -> 44.8 us  [local(): pl.pallas_call(functools.partial(kernel, nz, nf, layers, rows, heads), ou...]
where the time goes in v4:
time: 47.9 us; the launch traced here: 47.8 us
  Pallas kernels  47 us (98%)
  between operations  0.8 us (2%)
    pallas_call x1, Pallas kernels, local(): pl.pallas_call(functools.partial(kernel, nz, nf, layers, rows, heads), ou...  44.8 us
    pallas_call x1, Pallas kernels, local(): pl.pallas_call(functools.partial(finish, layers, rows, heads), out_shape=...  2.27 us

profile of v4, /device:TPU:1, one launch (start us, length us, event | category | flops | bytes accessed | tf_op | source)
XLA Modules:
  0.0 47.8 jit_solution(8211443896236778371)
XLA Ops:
  0.6 44.8 %backward.1 = (bf16[3,1024,256]{2,1,0:T(8,128)(2,1)S(1)}, f32[3,1024,256]{2,1,0:T(8,128)S(1)}, f32[3,1024,256]{2,1,0:T(8,128)S(1)}, bf16[3,1024,256]{2,1,0:T(8,1...) custom-call(bf16[3,1024,256]{2,1,0:T(8,128)(2,1)} %q_hbm.1, ...), custom_call_target="tpu_custom_call" | custom-call | tf_op jit(solution)/shard_map/backward/pallas_call | solution.py:560
  45.4 2.3 %finish.1 = (bf16[3,1024,256]{2,1,0:T(8,128)(2,1)}, bf16[3,1024,256]{2,1,0:T(8,128)(2,1)}, bf16[3,1024,256]{2,1,0:T(8,128)(2,1)}, f32[3,256]{1,0:T(4,128)}) custom-call(bf16[3,1024,256]{2,1,0:T(8,128)(2,1)S(1)} %get-tuple-element.11.dq_ref, f32[3,1024,256]{2,1,0:T(8,128)S(1)} %get-tuple-element.12.kpart, f32[3,1024,256]{2,1,0:T(8,128)S(1)} %get-tuple-element.13.vpart, ...), custom_call_target="tpu_custom_call" | custom-call | tf_op jit(solution)/shard_map/finish/pallas_call | solution.py:582

commit v5 on v4

--- a/solution.py
+++ b/solution.py
@@ -77,7 +77,7 @@
         remote(part, part, sem, sem, partner).wait_recv()
 
     def load(i, hbm, ref, l):
-        return pltpu.make_async_copy(hbm.at[l], ref.at[l], ld_sem.at[i, l])
+        return pltpu.make_async_copy(hbm.at[l], ref.at[l], ld_sem.at[l])
 
     small = (
         pltpu.make_async_copy(seg_hbm, seg_ref, small_sem.at[0]),
@@ -136,7 +136,7 @@
         return jnp.concatenate([column_mask(b, value)] * heads, axis=1)
 
     def hand_over(w, l):
-        remote(dsum.at[w, l, 1 - c], dpart.at[w, l], d_s.at[w], d_r.at[w, l], partner).start()
+        remote(dsum.at[w, l, 1 - c], dpart.at[w, l], d_s, d_r.at[w, l], partner).start()
 
     def chip_total(w, l, own_weight, partner_weight):
         arrived(dpart.at[w, l], d_r.at[w, l])
@@ -146,7 +146,7 @@
             at = pl.multiple_of(zmod(z + j) * cut, cut)
             into = b_r if j == opposite else a_r
             remote(
-                tot.at[w, l, pl.ds(at, cut)], slots.at[w, l, z], a_s.at[w], into.at[w, l], zpeer(j)
+                tot.at[w, l, pl.ds(at, cut)], slots.at[w, l, z], a_s, into.at[w, l], zpeer(j)
             ).start()
         slots[w, l, z] = tot[w, l, pl.ds(pl.multiple_of(z * cut, cut), cut)]
 
@@ -186,7 +186,7 @@
                 if far_use(r) == late:
                     ebuf[w, l, zmod(z + r)] = state(r)
                     remote(
-                        ebuf.at[w, l, zmod(z + r)], ein.at[w, l, here], e_s.at[w], e_r.at[w, l], zpeer(r)
+                        ebuf.at[w, l, zmod(z + r)], ein.at[w, l, here], e_s, e_r.at[w, l], zpeer(r)
                     ).start()
         ein[w, l, here] = state(0)
 
@@ -200,22 +200,21 @@
         own_add = jnp.where(second, zero + 1.0, zero)
         partner_add = jnp.where(second, zero, zero + 1.0)
         xbuf[w, l] = partner_weight * state + partner_add * dsum[w, l, c]
-        remote(xbuf.at[w, l], dev.at[w, l, c], x_s.at[w], x_r.at[w, l], partner).start()
+        remote(xbuf.at[w, l], dev.at[w, l, c], x_s, x_r.at[w, l], partner).start()
         dev[w, l, c] = own_weight * state + own_add * dpart[w, l]
 
     def entered(w, l):
         arrived(dev.at[w, l, 1 - c], x_r.at[w, l])
 
     def sent_state(w):
-        sent(dsum.at[w, :, 0], d_s.at[w])
-        sent(tot.at[w, :, 0 : DH - cut], a_s.at[w])
-        sent(ebuf.at[w, :, 0 : nz - 1], e_s.at[w])
-        sent(xbuf.at[w], x_s.at[w])
+        sent(dsum.at[w, :, 0], d_s)
+        sent(tot.at[w, :, 0 : DH - cut], a_s)
+        sent(ebuf.at[w, :, 0 : nz - 1], e_s)
+        sent(xbuf.at[w], x_s)
 
     tail_masks = [wide_mask(b, last[b]) for b in range(nb)]
     def tails_of(l, carry):
-        load(0, k_hbm, k_ref, l).wait()
-        load(1, v_hbm, v_ref, l).wait()
+        pltpu.make_async_copy(k_hbm.at[0:2], k_ref.at[0:2], ld_sem.at[l]).wait()
         totals = [None] * heads
         for b in range(nb):
             both = dot(k_ref[l, blk(b), :], v_ref[l, blk(b), :] * tail_masks[b], 0, 0)
@@ -353,6 +352,10 @@
             carried(l - 1)
     carried(layers - 1)
 
+    sent(mytile, tile_s)
+    sent(tabz.at[0 : nz - 1], tab_s)
+    sent_state(0)
+
     def gradient(l, carry):
         arrived(stat.at[l, 0 : nf - 1], st_r.at[l])
         summed = stat[l, 0]
@@ -373,13 +376,15 @@
             col_o = jnp.concatenate(
                 [jnp.broadcast_to(turned[:, 8 + per * b + i : 9 + per * b + i], (128, 128)) for i in range(per)], axis=0
             )
+            grads = []
             for h in range(heads):
                 o = o_ref[l, blk(b), hd(h)]
                 up = g_ref[l, blk(b), hd(h)].astype(F32) * col_a
                 gains[h] = gains[h] + jnp.sum(up * o, axis=0, keepdims=True)
-                grad = (up * gain8[l, 0:1, hd(h)] - o * col_o).astype(BF16)
-                do_ref[l, blk(b), hd(h)] = grad
-            both = dot(qmt[l, :, blk(b)], do_ref[l, blk(b), :], 1, 0)
+                grads.append((up * gain8[l, 0:1, hd(h)] - o * col_o).astype(BF16))
+            grad = jnp.concatenate(grads, axis=1)
+            do_ref[l, blk(b), :] = grad
+            both = dot(qmt[l, :, blk(b)], grad, 1, 0)
             for h in range(heads):
                 part = both[hd(h), hd(h)]
                 fronts[l, h, b] = part
@@ -461,9 +466,6 @@
         outer_q(l, 0)
         entering(1, l - 1, joined)
     store_dq.start()
-    sent(mytile, tile_s)
-    sent(tabz.at[0 : nz - 1], tab_s)
-    sent_state(0)
     sent(stat.at[:, 0 : nf - 1], st_s)
     sent(gtile, gt_s)
 
@@ -533,7 +535,7 @@
 
     near = pl.BlockSpec(memory_space=pltpu.VMEM)
     scratch = [
-        vmem(whole, BF16), vmem(whole, BF16), vmem(whole, BF16), vmem(whole, BF16), dma((2, layers)), dma((2,)),
+        vmem(whole, BF16), vmem(whole, BF16), vmem(whole, BF16), vmem(whole, BF16), dma((layers,)), dma((2,)),
         vmem((layers, channels), F32), vmem((rows // 128, 128), jnp.int32),
         pltpu.SMEM((layers,), jnp.int32), dma((4,)), dma((6,)),
         vmem(whole, BF16), vmem((layers, heads, nb, DH, DH), BF16), vmem((layers, channels), F32),
@@ -550,10 +552,10 @@
         vmem((layers, nf, 16, 128), F32), vmem((layers, 8, channels), F32), vmem((layers, heads, 8, DH), F32),
         vmem((8, 128), F32), vmem((8, 128), F32), vmem((nz, 8, 128), F32),
         dma, dma, dma, dma,
-        dma((2,)), dma((2, layers)),
-        dma((2,)), dma((2, layers)), dma((2, layers)),
-        dma((2,)), dma((2, layers)),
-        dma((2,)), dma((2, layers)),
+        dma, dma((2, layers)),
+        dma, dma((2, layers)), dma((2, layers)),
+        dma, dma((2, layers)),
+        dma, dma((2, layers)),
         dma, dma((layers,)),
         dma, dma, dma, dma,
     ]

time: 47.9 us -> 47.8 us (level)
  no operation moved by 1% of the time
where the time goes in v5:
time: 47.8 us; the launch traced here: 47.7 us
  Pallas kernels  46.9 us (98%)
  between operations  0.8 us (2%)
    pallas_call x1, Pallas kernels, local(): pl.pallas_call(functools.partial(kernel, nz, nf, layers, rows, heads), ou...  44.6 us
    pallas_call x1, Pallas kernels, local(): pl.pallas_call(functools.partial(finish, layers, rows, heads), out_shape=...  2.27 us

profile of v5, /device:TPU:1, one launch (start us, length us, event | category | flops | bytes accessed | tf_op | source)
XLA Modules:
  0.0 47.7 jit_solution(15580329618016041175)
XLA Ops:
  0.6 44.6 %backward.1 = (bf16[3,1024,256]{2,1,0:T(8,128)(2,1)S(1)}, f32[3,1024,256]{2,1,0:T(8,128)S(1)}, f32[3,1024,256]{2,1,0:T(8,128)S(1)}, bf16[3,1024,256]{2,1,0:T(8,1...) custom-call(bf16[3,1024,256]{2,1,0:T(8,128)(2,1)} %q_hbm.1, ...), custom_call_target="tpu_custom_call" | custom-call | tf_op jit(solution)/shard_map/backward/pallas_call | solution.py:562
  45.2 2.3 %finish.1 = (bf16[3,1024,256]{2,1,0:T(8,128)(2,1)}, bf16[3,1024,256]{2,1,0:T(8,128)(2,1)}, bf16[3,1024,256]{2,1,0:T(8,128)(2,1)}, f32[3,256]{1,0:T(4,128)}) custom-call(bf16[3,1024,256]{2,1,0:T(8,128)(2,1)S(1)} %get-tuple-element.11.dq_ref, f32[3,1024,256]{2,1,0:T(8,128)S(1)} %get-tuple-element.12.kpart, f32[3,1024,256]{2,1,0:T(8,128)S(1)} %get-tuple-element.13.vpart, ...), custom_call_target="tpu_custom_call" | custom-call | tf_op jit(solution)/shard_map/finish/pallas_call | solution.py:584
